TPU v7x, 512 devices: a whole 4x4x16 slice. The times are simulated.
512 devices in a mesh: frame: 16 (over x, z_lo), row: 8 (over z_hi, core), col: 4 (over y).
Axes of the slice: x: 4, y: 4, z: 16 (z_hi: 4, z_lo: 4; z = z_hi * 4 + z_lo), core: 2. Of those that a mesh axis runs over, the one named last changes fastest.
Arguments:
- query: bfloat16 [2048, 128, 640], P(('frame', 'row'), 'col'), parts along dimension 0, may hold values from -6 to 6, as said below
- keys: bfloat16 [2048, 128, 640], P(('frame', 'row'), 'col'), parts along dimension 0, may hold values from -6 to 6, as said below
- values: bfloat16 [2048, 128, 640], P(('frame', 'row'), 'col'), parts along dimension 0, may hold values from -6 to 6
- out_weight: bfloat16 [640, 1280], P(None, ('row', 'col')), may hold values from -0.25 to 0.25
Outputs:
- projected: bfloat16 [2048, 128, 1280], P(('frame', 'row'), 'col'), parts along dimension 0
There are 16 independent parts, one for each index of `frame`. A program takes and returns all parts, laid end to end along the dimension named above; an argument that names none is the same for every part. Nothing has to cross between parts.
Inputs may be any that keep to these rules, and one draw needn't show every extreme that they name: `query`: entries are real numbers of order one. `keys`: entries are real numbers of order one.
All inputs are finite; a program needn't handle non-finite values.
Results may differ from a plain program's by a relative error of at most 0.0056.
Values may be sent and summed in bfloat16 or wider, within the bound.
No kernel may reach another device: no remote copies, remote signals or barrier semaphores. Data moves between devices by JAX's collectives and lax.ppermute only.
A program may use at most 64 MiB of HBM per device.

v0:
```python
import jax
import jax.numpy as jnp
from jax import lax
from jax.sharding import PartitionSpec as P

HEADS = 8
HDIM = 80
BLOCK = 16


def shifted(block, axis, distance):
    devices = range(lax.axis_size(axis))
    route = [(i - distance, i) for i in devices if i - distance in devices]
    return lax.ppermute(block, axis, route)


def attend_block(query_block, key_block, value_block, upper_ok, left_ok):
    side = query_block.shape[0]
    chans = query_block.shape[2]
    q_heads = query_block.reshape(side * side, HEADS, HDIM)
    k_heads = key_block.reshape(4 * side * side, HEADS, HDIM)
    v_heads = value_block.reshape(4 * side * side, HEADS, HDIM)
    scores = jnp.einsum(
        "qhd,khd->hqk", q_heads, k_heads, preferred_element_type=jnp.float32
    ) * HDIM ** (-0.5)
    place = jnp.arange(4 * side * side, dtype=jnp.int32)
    in_upper = place // (2 * side) < side
    in_left = place % (2 * side) < side
    valid = jnp.logical_and(
        jnp.logical_or(jnp.logical_not(in_upper), upper_ok),
        jnp.logical_or(jnp.logical_not(in_left), left_ok),
    )
    scores = jnp.where(valid[None, None, :], scores, jnp.float32(-1e30))
    largest = jnp.max(scores, axis=-1, keepdims=True)
    weight = jnp.exp(scores - largest)
    total = jnp.sum(weight, axis=-1)
    rounded = weight.astype(jnp.bfloat16)
    mixed = jnp.einsum("hqk,khd->qhd", rounded, v_heads, preferred_element_type=jnp.float32)
    mixed = mixed / jnp.transpose(total)[:, :, None]
    return mixed.reshape(side * side, chans).astype(jnp.bfloat16)


def on_device(query, keys, values, out_weight):
    row_index = lax.axis_index("row")
    col_index = lax.axis_index("col")
    rows_dev, cols_dev, chans = query.shape
    band_rows = rows_dev // BLOCK
    band_cols = cols_dev // BLOCK
    left_k, left_v = shifted((keys[:, -BLOCK:], values[:, -BLOCK:]), "col", 1)
    upper_k, upper_v = shifted((keys, values), "row", 1)
    diag_k, diag_v = shifted((upper_k[:, -BLOCK:], upper_v[:, -BLOCK:]), "col", 1)
    top_k = jnp.concatenate([diag_k, upper_k], axis=1)
    top_v = jnp.concatenate([diag_v, upper_v], axis=1)
    ext_k = jnp.concatenate([top_k, jnp.concatenate([left_k, keys], axis=1)], axis=0)
    ext_v = jnp.concatenate([top_v, jnp.concatenate([left_v, values], axis=1)], axis=0)
    first_row = row_index * band_rows
    first_col = col_index * band_cols

    def one_block(index):
        brow = index // band_cols
        bcol = index % band_cols
        zero = jnp.zeros((), jnp.int32)
        query_block = lax.dynamic_slice(
            query, (brow * BLOCK, bcol * BLOCK, zero), (BLOCK, BLOCK, chans)
        )
        key_block = lax.dynamic_slice(
            ext_k, (brow * BLOCK, bcol * BLOCK, zero), (2 * BLOCK, 2 * BLOCK, chans)
        )
        value_block = lax.dynamic_slice(
            ext_v, (brow * BLOCK, bcol * BLOCK, zero), (2 * BLOCK, 2 * BLOCK, chans)
        )
        return attend_block(
            query_block, key_block, value_block, first_row + brow > 0, first_col + bcol > 0
        )

    attended = lax.map(one_block, jnp.arange(band_rows * band_cols, dtype=jnp.int32))
    flat = attended.reshape(band_rows * band_cols * BLOCK * BLOCK, chans)
    projected = jnp.dot(
        flat,
        lax.all_gather(out_weight, ("row", "col"), axis=1, tiled=True),
        preferred_element_type=jnp.float32,
    ).astype(jnp.bfloat16)
    width = projected.shape[1]
    projected = projected.reshape(band_rows, band_cols, BLOCK, BLOCK, width)
    projected = jnp.transpose(projected, (0, 2, 1, 3, 4))
    return projected.reshape(rows_dev, cols_dev, width)


def solution(mesh):
    placed = (
        P(("frame", "row"), "col", None),
        P(("frame", "row"), "col", None),
        P(("frame", "row"), "col", None),
        P(None, ("row", "col")),
    )
    return jax.shard_map(
        on_device,
        mesh=mesh,
        in_specs=placed,
        out_specs=P(("frame", "row"), "col", None),
        check_vma=False,
    )
```

profile of v0, /device:TPU:1, one launch (start us, length us, event | category | flops | bytes accessed | tf_op | source)
XLA Modules:
  0.0 166.7 jit_solution(5405335748459312961)
XLA Ops:
  6.5 10.3 %collective-permute-start.3 = (bf16[16,32,640]{2,1,0:T(8,128)(2,1)}, bf16[16,32,640]{2,1,0:T(8,128)(2,1)S(1)}, u32[]{:S(2)}, u32[]{:S(2)}) collective-permute-start(bf16[16,32,640]{2,1,0:T(8,128)(2,1)} %param.7), channel_id=1, source_target_pairs={{0,4},{4,8},{8,12},{12,16},{16,20},{20,24},{24,28},{1,5},{5,9},{9,... | collective-permute-start | bytes 1966088 | tf_op jit(solution)/shard_map/ppermute | solution.py:14
  19.8 4.0 %collective-permute-start.5 = (bf16[16,16,640]{2,1,0:T(8,128)(2,1)S(1)}, bf16[16,16,640]{2,1,0:T(8,128)(2,1)}, u32[]{:S(2)}, u32[]{:S(2)}) collective-permute-start(bf16[16,16,640]{2,1,0:T(8,128)(2,1)S(1)} %slice.15), channel_id=1, source_target_pairs={{0,1},{1,2},{2,3},{4,5},{5,6},{6,7},{8,9},{9,10},{10,11},{12,13},{... | collective-permute-start | bytes 983048 | tf_op jit(solution)/shard_map/ppermute | solution.py:14
  24.9 3.9 %collective-permute-start.4 = (bf16[16,16,640]{2,1,0:T(8,128)(2,1)S(1)}, bf16[16,16,640]{2,1,0:T(8,128)(2,1)}, u32[]{:S(2)}, u32[]{:S(2)}) collective-permute-start(bf16[16,16,640]{2,1,0:T(8,128)(2,1)S(1)} %slice.17), channel_id=1, source_target_pairs={{0,1},{1,2},{2,3},{4,5},{5,6},{6,7},{8,9},{9,10},{10,11},{12,13},{... | collective-permute-start | bytes 983048 | tf_op jit(solution)/shard_map/ppermute | solution.py:14
  29.8 3.2 %collective-permute-start.2 = (bf16[16,16,640]{2,1,0:T(8,128)(2,1)S(1)}, bf16[16,16,640]{2,1,0:T(8,128)(2,1)}, u32[]{:S(2)}, u32[]{:S(2)}) collective-permute-start(bf16[16,16,640]{2,1,0:T(8,128)(2,1)S(1)} %slice.13), channel_id=1, source_target_pairs={{0,1},{1,2},{2,3},{4,5},{5,6},{6,7},{8,9},{9,10},{10,11},{12,13},{... | collective-permute-start | bytes 983048 | tf_op jit(solution)/shard_map/ppermute | solution.py:14
  33.1 2.9 %collective-permute-start.1 = (bf16[16,16,640]{2,1,0:T(8,128)(2,1)S(1)}, bf16[16,16,640]{2,1,0:T(8,128)(2,1)}, u32[]{:S(2)}, u32[]{:S(2)}) collective-permute-start(bf16[16,16,640]{2,1,0:T(8,128)(2,1)S(1)} %slice.16), channel_id=1, source_target_pairs={{0,1},{1,2},{2,3},{4,5},{5,6},{6,7},{8,9},{9,10},{10,11},{12,13},{... | collective-permute-start | bytes 983048 | tf_op jit(solution)/shard_map/ppermute | solution.py:14
  36.6 2.8 %maximum_maximum_fusion.1 = bf16[32,48,640]{2,1,0:T(8,128)(2,1)} fusion(bf16[16,32,640]{2,1,0:T(8,128)(2,1)} %param.7, bf16[16,16,640]{2,1,0:T(8,128)(2,1)} %collective-permute-done.5, bf16[16,32,640]{2,1,0:T(8,128)(2,1)S(1)} %collective-permute-done.3, bf16[16,16,640]{2,1,0:T(8,128)(2,1)} %collective-permute-done.4), kind=kLoop, calls=%fused_computation.40 | loop fusion | flops 7864320 | bytes 3932160 | tf_op jit(solution)/shard_map/concatenate | solution.py:54
  39.3 4.3 %collective-permute-done.2 = bf16[16,16,640]{2,1,0:T(8,128)(2,1)} collective-permute-done((bf16[16,16,640]{2,1,0:T(8,128)(2,1)S(1)}, bf16[16,16,640]{2,1,0:T(8,128)(2,1)}, u32[]{:S(2)}, u32[]{:S(2)}) %collective-permute-start.2) | collective-permute-done | bytes 327712 | tf_op jit(solution)/shard_map/ppermute | solution.py:14
  43.6 7.0 %collective-permute-done.1 = bf16[16,16,640]{2,1,0:T(8,128)(2,1)} collective-permute-done((bf16[16,16,640]{2,1,0:T(8,128)(2,1)S(1)}, bf16[16,16,640]{2,1,0:T(8,128)(2,1)}, u32[]{:S(2)}, u32[]{:S(2)}) %collective-permute-start.1) | collective-permute-done | bytes 327712 | tf_op jit(solution)/shard_map/ppermute | solution.py:14
  50.6 2.5 %maximum_maximum_fusion = bf16[32,48,640]{2,1,0:T(8,128)(2,1)} fusion(bf16[16,32,640]{2,1,0:T(8,128)(2,1)S(1)} %copy-done.1, bf16[16,16,640]{2,1,0:T(8,128)(2,1)} %collective-permute-done.2, bf16[16,32,640]{2,1,0:T(8,128)(2,1)S(1)} %collective-permute-done, bf16[16,16,640]{2,1,0:T(8,128)(2,1)} %collective-permute-done.1), kind=kLoop, calls=%fused_computation.39 | loop fusion | flops 7864320 | bytes 3932160 | tf_op jit(solution)/shard_map/concatenate | solution.py:55
  53.1 57.1 %while.13 = (s32[]{:T(128)}, bf16[2,256,640]{2,1,0:T(8,128)(2,1)}, s32[2]{0:T(128)S(1)}, bf16[32,48,640]{2,1,0:T(8,128)(2,1)}, s32[]{:T(128)}, /*index=5*/s32[]{...) while((s32[]{:T(128)}, bf16[2,256,640]{2,1,0:T(8,128)(2,1)}, ...), condition=%wide.region_3.4_spmd, body=%wide.region_0.3_spmd.sunk | while | flops 694500352 | bytes 80392744 | solution.py:76
  55.6 3.0 %constant_dynamic-slice_fusion.5 = (bf16[32,32,640]{2,1,0:T(8,128)(2,1)}, bf16[32,32,640]{2,1,0:T(8,128)(2,1)S(1)}) fusion(bf16[32,48,640]{2,1,0:T(8,128)(2,1)} %get-tuple-element.269, s32[]{:T(128)S(6)} %select_n.126, bf16[32,48,640]{2,1,0:T(8,128)(2,1)} %get-tuple-element.265), kind=kLoop, calls=%fused_computation.33.clone.1 | loop fusion | bytes 5242884 | tf_op jit(solution)/shard_map/while/body/eval_jaxpr/dynamic_slice | solution.py:66
  58.6 3.7 %reshape.81 = bf16[1024,8,80]{2,1,0:T(8,128)(2,1)S(1)} reshape(bf16[32,32,640]{2,1,0:T(8,128)(2,1)} %get-tuple-element.228) | data formatting | bytes 2621440 | tf_op jit(solution)/shard_map/while/body/eval_jaxpr/reshape | solution.py:21
  64.1 2.3 %reshape.82 = bf16[256,8,80]{2,1,0:T(8,128)(2,1)} reshape(bf16[16,16,640]{2,1,0:T(8,128)(2,1)} %constant_dynamic-slice_fusion.6) | data formatting | bytes 655360 | tf_op jit(solution)/shard_map/while/body/eval_jaxpr/reshape | solution.py:20
  67.1 2.6 %fusion.52 = (f32[8,256]{1,0:T(8,128)S(1)}, f32[8,256,1024]{2,1,0:T(8,128)S(1)}) fusion(pred[1024]{0:T(1024)(128)(4,1)S(1)} %fusion.51, bf16[1024,8,80]{2,1,0:T(8,128)(2,1)S(1)} %reshape.81, bf16[256,8,80]{2,1,0:T(8,128)(2,1)} %reshape.82), kind=kOutput, calls=%fused_computation.2.clone.1 | convolution fusion | flops 341833728 | bytes 10036224 | tf_op jit(solution)/shard_map/while/body/eval_jaxpr/qhd,khd->hqk/dot_general | solution.py:23
  72.9 2.1 %reshape.83 = bf16[1024,8,80]{2,1,0:T(8,128)(2,1)S(1)} reshape(bf16[32,32,640]{2,1,0:T(8,128)(2,1)S(1)} %get-tuple-element.231) | data formatting | bytes 2621440 | tf_op jit(solution)/shard_map/while/body/eval_jaxpr/reshape | solution.py:22
  75.0 5.5 %fusion.54 = bf16[256,8,80]{0,2,1:T(8,128)(2,1)S(1)} fusion(f32[8,256,1024]{2,1,0:T(8,128)} %copy-done, f32[8,256]{1,0:T(8,128)S(1)} %get-tuple-element.230, pred[1024]{0:T(1024)(128)(4,1)S(1)} %fusion.51, bf16[1024,8,80]{2,1,0:T(8,128)(2,1)S(1)} %reshape.83, f32[256,8]{0,1:T(8,128)S(1)} %bitcast.26), kind=kOutput, calls=%fused_computation.12.clone.1 | convolution fusion | flops 344260608 | bytes 10044416 | tf_op jit(solution)/shard_map/while/body/eval_jaxpr/hqk,khd->qhd/dot_general | solution.py:38
  84.2 3.0 %constant_dynamic-slice_fusion.5 = (bf16[32,32,640]{2,1,0:T(8,128)(2,1)}, bf16[32,32,640]{2,1,0:T(8,128)(2,1)S(1)}) fusion(bf16[32,48,640]{2,1,0:T(8,128)(2,1)} %get-tuple-element.269, s32[]{:T(128)S(6)} %select_n.126, bf16[32,48,640]{2,1,0:T(8,128)(2,1)} %get-tuple-element.265), kind=kLoop, calls=%fused_computation.33.clone.1 | loop fusion | bytes 5242884 | tf_op jit(solution)/shard_map/while/body/eval_jaxpr/dynamic_slice | solution.py:66
  87.2 3.7 %reshape.81 = bf16[1024,8,80]{2,1,0:T(8,128)(2,1)S(1)} reshape(bf16[32,32,640]{2,1,0:T(8,128)(2,1)} %get-tuple-element.228) | data formatting | bytes 2621440 | tf_op jit(solution)/shard_map/while/body/eval_jaxpr/reshape | solution.py:21
  92.6 2.3 %reshape.82 = bf16[256,8,80]{2,1,0:T(8,128)(2,1)} reshape(bf16[16,16,640]{2,1,0:T(8,128)(2,1)} %constant_dynamic-slice_fusion.6) | data formatting | bytes 655360 | tf_op jit(solution)/shard_map/while/body/eval_jaxpr/reshape | solution.py:20
  95.6 2.6 %fusion.52 = (f32[8,256]{1,0:T(8,128)S(1)}, f32[8,256,1024]{2,1,0:T(8,128)S(1)}) fusion(pred[1024]{0:T(1024)(128)(4,1)S(1)} %fusion.51, bf16[1024,8,80]{2,1,0:T(8,128)(2,1)S(1)} %reshape.81, bf16[256,8,80]{2,1,0:T(8,128)(2,1)} %reshape.82), kind=kOutput, calls=%fused_computation.2.clone.1 | convolution fusion | flops 341833728 | bytes 10036224 | tf_op jit(solution)/shard_map/while/body/eval_jaxpr/qhd,khd->hqk/dot_general | solution.py:23
  101.5 2.1 %reshape.83 = bf16[1024,8,80]{2,1,0:T(8,128)(2,1)S(1)} reshape(bf16[32,32,640]{2,1,0:T(8,128)(2,1)S(1)} %get-tuple-element.231) | data formatting | bytes 2621440 | tf_op jit(solution)/shard_map/while/body/eval_jaxpr/reshape | solution.py:22
  103.6 5.5 %fusion.54 = bf16[256,8,80]{0,2,1:T(8,128)(2,1)S(1)} fusion(f32[8,256,1024]{2,1,0:T(8,128)} %copy-done, f32[8,256]{1,0:T(8,128)S(1)} %get-tuple-element.230, pred[1024]{0:T(1024)(128)(4,1)S(1)} %fusion.51, bf16[1024,8,80]{2,1,0:T(8,128)(2,1)S(1)} %reshape.83, f32[256,8]{0,1:T(8,128)S(1)} %bitcast.26), kind=kOutput, calls=%fused_computation.12.clone.1 | convolution fusion | flops 344260608 | bytes 10044416 | tf_op jit(solution)/shard_map/while/body/eval_jaxpr/hqk,khd->qhd/dot_general | solution.py:38
  110.2 45.6 %all-gather.2.cloned.1.call-done = bf16[640,1280]{0,1:T(8,128)(2,1)} async-done(((bf16[640,40]{0,1:T(8,128)(2,1)}), bf16[640,1280]{0,1:T(8,128)(2,1)}) %all-gather.2.cloned.1.call-update) | async-done | bytes 1638416 | tf_op jit(solution)/shard_map/all_gather | solution.py:80
  155.8 2.9 %convolution_convert_fusion = bf16[512,1280]{1,0:T(8,128)(2,1)S(1)} fusion(bf16[512,640]{1,0:T(8,128)(2,1)} %bitcast.27, bf16[640,1280]{0,1:T(8,128)(2,1)} %all-gather.2.cloned.1.call-done), kind=kOutput, calls=%fused_computation.38 | convolution fusion | flops 839516160 | bytes 3604480 | tf_op jit(solution)/shard_map/dot_general | solution.py:78
  (40 shorter events, 20.1 us)
Async XLA Ops:
  6.5 44.1 %copy-start.1 = (bf16[16,32,640]{2,1,0:T(8,128)(2,1)S(1)}, bf16[16,32,640]{2,1,0:T(8,128)(2,1)}, u32[]{:S(2)}) copy-start(bf16[16,32,640]{2,1,0:T(8,128)(2,1)} %param.8) | copy-start | bytes 1966084
  6.5 149.3 %all-gather.2.cloned.1.call-start = ((), (), s32[]{:S(2)}) async-start(), calls=%async_computation | async-start | bytes 1689600 | tf_op jit(solution)/shard_map/all_gather | solution.py:80
  6.5 18.3 %collective-permute-start.3 = (bf16[16,32,640]{2,1,0:T(8,128)(2,1)}, bf16[16,32,640]{2,1,0:T(8,128)(2,1)S(1)}, u32[]{:S(2)}, u32[]{:S(2)}) collective-permute-start(bf16[16,32,640]{2,1,0:T(8,128)(2,1)} %param.7), channel_id=1, source_target_pairs={{0,4},{4,8},{8,12},{12,16},{16,20},{20,24},{24,28},{1,5},{5,9},{9,... | collective-permute-start | bytes 1966088 | tf_op jit(solution)/shard_map/ppermute | solution.py:14
  16.9 16.2 %collective-permute-start = (bf16[16,32,640]{2,1,0:T(8,128)(2,1)}, bf16[16,32,640]{2,1,0:T(8,128)(2,1)S(1)}, u32[]{:S(2)}, u32[]{:S(2)}) collective-permute-start(bf16[16,32,640]{2,1,0:T(8,128)(2,1)} %param.8), channel_id=1, source_target_pairs={{0,4},{4,8},{8,12},{12,16},{16,20},{20,24},{24,28},{1,5},{5,9},{9,... | collective-permute-start | bytes 1966088 | tf_op jit(solution)/shard_map/ppermute | solution.py:14
  19.8 16.2 %collective-permute-start.5 = (bf16[16,16,640]{2,1,0:T(8,128)(2,1)S(1)}, bf16[16,16,640]{2,1,0:T(8,128)(2,1)}, u32[]{:S(2)}, u32[]{:S(2)}) collective-permute-start(bf16[16,16,640]{2,1,0:T(8,128)(2,1)S(1)} %slice.15), channel_id=1, source_target_pairs={{0,1},{1,2},{2,3},{4,5},{5,6},{6,7},{8,9},{9,10},{10,11},{12,13},{... | collective-permute-start | bytes 983048 | tf_op jit(solution)/shard_map/ppermute | solution.py:14
  24.9 11.7 %collective-permute-start.4 = (bf16[16,16,640]{2,1,0:T(8,128)(2,1)S(1)}, bf16[16,16,640]{2,1,0:T(8,128)(2,1)}, u32[]{:S(2)}, u32[]{:S(2)}) collective-permute-start(bf16[16,16,640]{2,1,0:T(8,128)(2,1)S(1)} %slice.17), channel_id=1, source_target_pairs={{0,1},{1,2},{2,3},{4,5},{5,6},{6,7},{8,9},{9,10},{10,11},{12,13},{... | collective-permute-start | bytes 983048 | tf_op jit(solution)/shard_map/ppermute | solution.py:14
  29.8 13.8 %collective-permute-start.2 = (bf16[16,16,640]{2,1,0:T(8,128)(2,1)S(1)}, bf16[16,16,640]{2,1,0:T(8,128)(2,1)}, u32[]{:S(2)}, u32[]{:S(2)}) collective-permute-start(bf16[16,16,640]{2,1,0:T(8,128)(2,1)S(1)} %slice.13), channel_id=1, source_target_pairs={{0,1},{1,2},{2,3},{4,5},{5,6},{6,7},{8,9},{9,10},{10,11},{12,13},{... | collective-permute-start | bytes 983048 | tf_op jit(solution)/shard_map/ppermute | solution.py:14
  33.1 17.6 %collective-permute-start.1 = (bf16[16,16,640]{2,1,0:T(8,128)(2,1)S(1)}, bf16[16,16,640]{2,1,0:T(8,128)(2,1)}, u32[]{:S(2)}, u32[]{:S(2)}) collective-permute-start(bf16[16,16,640]{2,1,0:T(8,128)(2,1)S(1)} %slice.16), channel_id=1, source_target_pairs={{0,1},{1,2},{2,3},{4,5},{5,6},{6,7},{8,9},{9,10},{10,11},{12,13},{... | collective-permute-start | bytes 983048 | tf_op jit(solution)/shard_map/ppermute | solution.py:14
  69.7 3.2 %copy-start = (f32[8,256,1024]{2,1,0:T(8,128)}, f32[8,256,1024]{2,1,0:T(8,128)S(1)}, u32[]{:S(2)}) copy-start(f32[8,256,1024]{2,1,0:T(8,128)S(1)} %get-tuple-element.229) | copy-start | bytes 25165828 | tf_op jit(solution)/shard_map/while
  75.0 5.8 %copy-start.2 = (bf16[2,256,640]{2,1,0:T(8,128)(2,1)S(1)}, bf16[2,256,640]{2,1,0:T(8,128)(2,1)}, u32[]{:S(2)}) copy-start(bf16[2,256,640]{2,1,0:T(8,128)(2,1)} %get-tuple-element.248) | copy-start | bytes 1966084 | tf_op jit(solution)/shard_map/while
  80.8 0.8 copy-start.3
  98.2 3.2 %copy-start = (f32[8,256,1024]{2,1,0:T(8,128)}, f32[8,256,1024]{2,1,0:T(8,128)S(1)}, u32[]{:S(2)}) copy-start(f32[8,256,1024]{2,1,0:T(8,128)S(1)} %get-tuple-element.229) | copy-start | bytes 25165828 | tf_op jit(solution)/shard_map/while
  103.6 5.8 %copy-start.2 = (bf16[2,256,640]{2,1,0:T(8,128)(2,1)S(1)}, bf16[2,256,640]{2,1,0:T(8,128)(2,1)}, u32[]{:S(2)}) copy-start(bf16[2,256,640]{2,1,0:T(8,128)(2,1)} %get-tuple-element.248) | copy-start | bytes 1966084 | tf_op jit(solution)/shard_map/while
  109.4 0.8 copy-start.3
Sparse Core Ops, SparseCore 0:
  36.1 119.6 all-gather.1
where the time goes:
time: 168 us; the launch traced here: 167 us
  waiting for transfers between devices  58.5 us (35%)
  local copies, waits for them, and re-layouts  34.9 us (21%)
  starting transfers between devices  26.3 us (16%)
  matrix products  19.1 us (11%)
  between operations  13.5 us (8%)
  other arithmetic  9.31 us (6%)
  loops' own time  5.2 us (3%)
    all_gather x1, waiting for transfers between devices, on_device(): lax.all_gather(out_weight, ('row', 'col'), axis=1, tiled=True)  45.6 us
    ppermute x6, starting transfers between devices, shifted(): return lax.ppermute(block, axis, route)  26.3 us
    ppermute x6, waiting for transfers between devices, shifted(): return lax.ppermute(block, axis, route)  12.9 us
    dot_general x2, matrix products, attend_block(): jnp.einsum('hqk,khd->qhd', rounded, v_heads, preferred_element_type=jnp.f...  11.1 us
    reshape x2, local copies, waits for them, and re-layouts, attend_block(): k_heads = key_block.reshape(4 * side * side, HEADS, HDIM)  7.37 us
    dynamic_slice x2, local copies, waits for them, and re-layouts, one_block(): lax.dynamic_slice(ext_k, (brow * BLOCK, bcol * BLOCK, zero), (2 * BLOCK,...  6.08 us
    another operation x1, loops' own time, on_device(): lax.map(one_block, jnp.arange(band_rows * band_cols, dtype=jnp.int32))  5.2 us
    dot_general x2, matrix products, attend_block(): jnp.einsum('qhd,khd->hqk', q_heads, k_heads, preferred_element_type=jnp.f...  5.19 us
  transfers between devices with their start and end apart: 7, of which 5 were waited for; matrix products, arithmetic and copies ran while one was open for 33% of the time, Pallas kernels for 0%

commit v1 on v0

v1 whole, which is shorter than its diff:
```python
import functools
import math

import jax
import jax.numpy as jnp
from jax import lax
from jax.experimental import pallas as pl
from jax.experimental.pallas import tpu as pltpu
from jax.sharding import PartitionSpec as P

HEADS = 8
HDIM = 80
BLOCK = 16
TOKENS = BLOCK * BLOCK
CHANNELS = HEADS * HDIM
SCALE = math.log2(math.e) * HDIM ** (-0.5)
NEG = -1e30
PACKED = CHANNELS + 32
SIDE = 4
AXES = ("frame", "row", "col")


def routed(block, target):
    route = []
    for x in range(SIDE):
        for zl in range(SIDE):
            for zh in range(SIDE):
                for core in range(2):
                    for y in range(SIDE):
                        to = target(x, zl, zh, core, y)
                        if to is not None:
                            route.append((place(x, zl, zh, core, y), place(*to)))
    return lax.ppermute(block, AXES, route)


def place(x, zl, zh, core, y):
    return ((x * SIDE + zl) * 2 * SIDE + zh * 2 + core) * SIDE + y


def shifted(block, axis, distance):
    devices = range(lax.axis_size(axis))
    route = [(i - distance, i) for i in devices if i - distance in devices]
    return lax.ppermute(block, axis, route)


def head_scores(keys, query_t, head):
    first = head * HDIM
    low = first // 128 * 128
    high = -(-(first + HDIM) // 128) * 128
    parts = []
    if first > low:
        parts.append(jnp.zeros((first - low, TOKENS), jnp.bfloat16))
    parts.append(query_t[first : first + HDIM])
    if high > first + HDIM:
        parts.append(jnp.zeros((high - first - HDIM, TOKENS), jnp.bfloat16))
    masked = jnp.concatenate(parts, axis=0)
    return jnp.dot(keys[:, low:high], masked, preferred_element_type=jnp.float32)


def attend(query_t, keys_a, keys_b, values_a, values_b, bias, emit):
    for head in range(HEADS):
        rows = slice(head * HDIM, (head + 1) * HDIM)
        score_a = head_scores(keys_a, query_t, head)
        score_b = head_scores(keys_b, query_t, head)
        if bias is not None:
            score_a = score_a + bias
        largest = jnp.maximum(
            jnp.max(score_a, axis=0, keepdims=True), jnp.max(score_b, axis=0, keepdims=True)
        )
        largest = largest * SCALE
        weight_a = jnp.exp2(score_a * SCALE - largest)
        weight_b = jnp.exp2(score_b * SCALE - largest)
        total = jnp.sum(weight_a, axis=0, keepdims=True) + jnp.sum(weight_b, axis=0, keepdims=True)
        mixed = jnp.dot(
            values_a[rows], weight_a.astype(jnp.bfloat16), preferred_element_type=jnp.float32
        ) + jnp.dot(
            values_b[rows], weight_b.astype(jnp.bfloat16), preferred_element_type=jnp.float32
        )
        emit(head, rows, mixed, largest, total)


def block_of(ref, col):
    return ref[:, col * BLOCK : (col + 1) * BLOCK, :].reshape(TOKENS, CHANNELS)


def left_bias():
    return jnp.where(lax.axis_index("col") > 0, jnp.float32(0.0), jnp.float32(NEG))


def own_kernel(query, keys, values, mixed_out, stats_out, values_t):
    values_t[0] = block_of(values, 0).T
    values_t[1] = block_of(values, 1).T

    def emit(head, rows, mixed, largest, total):
        mixed_out[rows] = mixed
        stats_out[head : head + 1] = largest
        stats_out[HEADS + head : HEADS + head + 1] = total

    attend(
        block_of(query, 1).T, block_of(keys, 0), block_of(keys, 1),
        values_t.at[0], values_t.at[1], None, emit,
    )


def edge_kernel(query, keys, left, values_t, mixed_out, stats_out, left_t):
    left_t[...] = left[BLOCK:].reshape(TOKENS, CHANNELS).T

    def emit(head, rows, mixed, largest, total):
        mixed_out[rows] = mixed
        stats_out[head : head + 1] = largest
        stats_out[HEADS + head : HEADS + head + 1] = total

    attend(
        block_of(query, 0).T, left[:BLOCK].reshape(TOKENS, CHANNELS), block_of(keys, 0),
        left_t, values_t.at[0], left_bias(), emit,
    )


def packing(packed, lse):
    def emit(head, rows, mixed, largest, total):
        packed[rows] = (mixed * (1.0 / total)).astype(jnp.bfloat16)
        lse[head : head + 1] = largest + jnp.log2(total)

    return emit


def pack_lse(packed, lse):
    whole = lse[...]
    high = whole.astype(jnp.bfloat16)
    rest = whole - high.astype(jnp.float32)
    middle = rest.astype(jnp.bfloat16)
    low = (rest - middle.astype(jnp.float32)).astype(jnp.bfloat16)
    packed[CHANNELS : CHANNELS + 16] = jnp.concatenate(
        [high.astype(jnp.float32), middle.astype(jnp.float32)], axis=0
    ).astype(jnp.bfloat16)
    packed[CHANNELS + 16 : CHANNELS + 32] = jnp.concatenate(
        [low.astype(jnp.float32), jnp.zeros_like(whole)], axis=0
    ).astype(jnp.bfloat16)


def lower_own_kernel(query, keys, values_t, packed, lse):
    attend(
        block_of(query, 1).T, block_of(keys, 0), block_of(keys, 1),
        values_t.at[0], values_t.at[1], None, packing(packed, lse),
    )
    pack_lse(packed, lse)


def lower_edge_kernel(query, keys, left, values_t, left_t, packed, lse):
    attend(
        block_of(query, 0).T, left[:BLOCK].reshape(TOKENS, CHANNELS), block_of(keys, 0),
        left_t, values_t.at[0], left_bias(), packing(packed, lse),
    )
    pack_lse(packed, lse)


def project_kernel(
    mixed_0, mixed_1, stats_0, stats_1, upper_0, upper_1, weight, other, projected, full, merged
):
    frame, row = lax.axis_index("frame"), lax.axis_index("row")
    x, z_hi, core = frame // SIDE, row // 2, row % 2
    span = SIDE * weight.shape[0] // (SIDE * SIDE)
    for item in range(SIDE):
        holder = lax.rem(z_hi + lax.rem(x + item, SIDE), SIDE) * 2
        for source, which in ((weight, core), (other, 1 - core)):
            start = pl.multiple_of((holder + which) * span, span)
            full[pl.ds(start, span)] = source[item * span : (item + 1) * span]
    has_upper = row > 0
    for col, (mixed, stats, upper) in enumerate(
        ((mixed_0, stats_0, upper_0), (mixed_1, stats_1, upper_1))
    ):
        largest, total = stats[:HEADS], stats[HEADS:]
        parts = upper[CHANNELS : CHANNELS + 32].astype(jnp.float32)
        lse = parts[:HEADS] + parts[HEADS : 2 * HEADS] + parts[2 * HEADS : 3 * HEADS]
        lse = jnp.where(has_upper, lse, jnp.float32(NEG))
        top = jnp.maximum(largest, lse)
        own_w = jnp.exp2(largest - top)
        upper_w = jnp.exp2(lse - top)
        share = 1.0 / (total * own_w + upper_w)
        own_w, upper_w = own_w * share, upper_w * share
        for head in range(HEADS):
            rows = slice(head * HDIM, (head + 1) * HDIM)
            merged[rows] = (
                mixed[rows] * own_w[head : head + 1]
                + upper[rows].astype(jnp.float32) * upper_w[head : head + 1]
            ).astype(jnp.bfloat16)
        result = lax.dot_general(
            merged[...].T, full[...], (((1,), (1,)), ((), ())), preferred_element_type=jnp.float32
        )
        projected[:, col * BLOCK : (col + 1) * BLOCK, :] = result.astype(jnp.bfloat16).reshape(
            BLOCK, BLOCK, projected.shape[2]
        )


def call(kernel, outs, scratch=(), flops=0, name=None):
    return pl.pallas_call(
        kernel,
        out_shape=outs,
        scratch_shapes=list(scratch),
        compiler_params=pltpu.CompilerParams(vmem_limit_bytes=32 * 1024 * 1024),
        cost_estimate=pl.CostEstimate(flops=flops, bytes_accessed=4_000_000, transcendentals=0),
        name=name,
    )


def gathered_weight(shard):
    item = routed(shard, lambda x, zl, zh, c, y: (x, zl, (zh - x) % SIDE, c, y))
    turns = [item] + [
        routed(item, lambda x, zl, zh, c, y: (x, zl, zh, c, (y - j) % SIDE)) for j in range(1, SIDE)
    ]
    ring = jnp.concatenate(turns + turns[:-1], axis=0)
    start = lax.rem(SIDE - lax.axis_index("col"), SIDE) * shard.shape[0]
    quarter = lax.dynamic_slice_in_dim(ring, start, SIDE * shard.shape[0], axis=0)
    items = [quarter] + [
        routed(quarter, lambda x, zl, zh, c, y: ((x - j) % SIDE, zl, zh, c, y))
        for j in range(1, SIDE)
    ]
    half = jnp.concatenate(items, axis=0)
    return half, routed(half, lambda x, zl, zh, c, y: (x, zl, zh, 1 - c, y))


def on_device(query, keys, values, out_weight):
    rows_dev, cols_dev, chans = query.shape
    width = out_weight.shape[1] * lax.axis_size("row") * lax.axis_size("col")
    lower_query = shifted(query, "row", -1)
    left = shifted(
        jnp.concatenate([keys[:, -BLOCK:], values[:, -BLOCK:]], axis=0), "col", 1
    )
    weight, other = gathered_weight(out_weight.T)

    f32, bf16 = jnp.float32, jnp.bfloat16
    mixed_s = jax.ShapeDtypeStruct((CHANNELS, TOKENS), f32)
    stats_s = jax.ShapeDtypeStruct((2 * HEADS, TOKENS), f32)
    packed_s = jax.ShapeDtypeStruct((PACKED, TOKENS), bf16)
    lse = pltpu.VMEM((HEADS, TOKENS), f32)
    flops = 4 * HEADS * TOKENS * 2 * TOKENS * 256

    mixed_1, stats_1, values_t = call(
        own_kernel, (mixed_s, stats_s, jax.ShapeDtypeStruct((2, CHANNELS, TOKENS), bf16)),
        flops=flops, name="own",
    )(query, keys, values)
    mixed_0, stats_0, left_t = call(
        edge_kernel, (mixed_s, stats_s, jax.ShapeDtypeStruct((CHANNELS, TOKENS), bf16)),
        flops=flops, name="edge",
    )(query, keys, left, values_t)
    packed_1 = call(lower_own_kernel, packed_s, (lse,), flops=flops, name="lower_own")(
        lower_query, keys, values_t
    )
    upper_1 = shifted(packed_1, "row", 1)
    packed_0 = call(lower_edge_kernel, packed_s, (lse,), flops=flops, name="lower_edge")(
        lower_query, keys, left, values_t, left_t
    )
    upper_0 = shifted(packed_0, "row", 1)
    return call(
        project_kernel,
        jax.ShapeDtypeStruct((rows_dev, cols_dev, width), bf16),
        (pltpu.VMEM((width, chans), bf16), pltpu.VMEM((CHANNELS, TOKENS), bf16)),
        flops=2 * 2 * TOKENS * CHANNELS * width, name="project",
    )(mixed_0, mixed_1, stats_0, stats_1, upper_0, upper_1, weight, other)


def solution(mesh):
    placed = (
        P(("frame", "row"), "col", None),
        P(("frame", "row"), "col", None),
        P(("frame", "row"), "col", None),
        P(None, ("row", "col")),
    )
    return jax.shard_map(
        on_device,
        mesh=mesh,
        in_specs=placed,
        out_specs=P(("frame", "row"), "col", None),
        check_vma=False,
    )
```

time: 168 us -> 101 us (0.60)
  the two profiles are of different devices: /device:TPU:1 before, /device:TPU:103 now
where the time goes in v1:
time: 101 us; the launch traced here: 100 us
  starting transfers between devices  48.7 us (48%)
  waiting for transfers between devices  36.1 us (36%)
  Pallas kernels  14.8 us (15%)
    ppermute x8, starting transfers between devices, routed(): return lax.ppermute(block, AXES, route)  35.5 us
    ppermute x4, waiting for transfers between devices, shifted(): return lax.ppermute(block, axis, route)  24.6 us
    ppermute x4, starting transfers between devices, shifted(): return lax.ppermute(block, axis, route)  13.2 us
    ppermute x8, waiting for transfers between devices, routed(): return lax.ppermute(block, AXES, route)  11.5 us
    pallas_call x1, Pallas kernels, on_device(): call(own_kernel, (mixed_s, stats_s, jax.ShapeDtypeStruct((2, CHANNELS, TO...  3.17 us
    pallas_call x1, Pallas kernels, on_device(): call(edge_kernel, (mixed_s, stats_s, jax.ShapeDtypeStruct((CHANNELS, TOKE...  3.17 us
    pallas_call x1, Pallas kernels, on_device(): call(lower_edge_kernel, packed_s, (lse,), flops=flops, name='lower_edge')  3.02 us
    pallas_call x1, Pallas kernels, on_device(): call(lower_own_kernel, packed_s, (lse,), flops=flops, name='lower_own')  3.01 us
  transfers between devices with their start and end apart: 12, of which 5 were waited for; matrix products, arithmetic and copies ran while one was open for 0% of the time, Pallas kernels for 12%

profile of v1, /device:TPU:103, one launch (start us, length us, event | category | flops | bytes accessed | tf_op | source)
XLA Modules:
  0.0 100.2 jit_solution(15243313584744439670)
XLA Ops:
  0.0 8.9 %collective-permute-start.4 = (bf16[40,640]{1,0:T(8,128)(2,1)}, bf16[40,640]{1,0:T(8,128)(2,1)S(1)}, u32[]{:S(2)}, u32[]{:S(2)}) collective-permute-start(bf16[40,640]{1,0:T(8,128)(2,1)} %bitcast.1), channel_id=1, source_target_pairs={{0,0},{1,1},{2,2},{3,3},{4,4},{5,5},{6,6},{7,7},{8,8},{9,9},{10,10... | collective-permute-start | bytes 153608 | tf_op jit(solution)/shard_map/ppermute | solution.py:33
  9.0 0.1 pad_maximum_fusion.1
  9.1 3.2 %collective-permute-start = (bf16[32,16,640]{2,1,0:T(8,128)(2,1)S(1)}, bf16[32,16,640]{2,1,0:T(8,128)(2,1)S(1)}, u32[]{:S(2)}, u32[]{:S(2)}) collective-permute-start(bf16[32,16,640]{2,1,0:T(8,128)(2,1)S(1)} %pad_maximum_fusion.1), channel_id=1, source_target_pairs={{0,1},{1,2},{2,3},{4,5},{5,6},{6,7},{8,9},{9,10},{10,11},{12,13},{... | collective-permute-start | bytes 1966088 | tf_op jit(solution)/shard_map/ppermute | solution.py:43
  12.3 3.1 %collective-permute-start.1 = (bf16[16,32,640]{2,1,0:T(8,128)(2,1)S(1)}, bf16[16,32,640]{2,1,0:T(8,128)(2,1)S(1)}, u32[]{:S(2)}, u32[]{:S(2)}) collective-permute-start(bf16[16,32,640]{2,1,0:T(8,128)(2,1)S(1)} %copy-done.2), channel_id=1, source_target_pairs={{4,0},{8,4},{12,8},{16,12},{20,16},{24,20},{28,24},{5,1},{9,5},{13... | collective-permute-start | bytes 1966088 | tf_op jit(solution)/shard_map/ppermute | solution.py:43
  15.5 4.4 %collective-permute-start.5 = (bf16[40,640]{1,0:T(8,128)(2,1)S(1)}, bf16[40,640]{1,0:T(8,128)(2,1)S(1)}, u32[]{:S(2)}, u32[]{:S(2)}) collective-permute-start(bf16[40,640]{1,0:T(8,128)(2,1)S(1)} %collective-permute-done.4), channel_id=1, source_target_pairs={{0,3},{1,0},{2,1},{3,2},{4,7},{5,4},{6,5},{7,6},{8,11},{9,8},{10,9... | collective-permute-start | bytes 153608 | tf_op jit(solution)/shard_map/ppermute | solution.py:33
  19.9 2.6 %collective-permute-start.6 = (bf16[40,640]{1,0:T(8,128)(2,1)S(1)}, bf16[40,640]{1,0:T(8,128)(2,1)S(1)}, u32[]{:S(2)}, u32[]{:S(2)}) collective-permute-start(bf16[40,640]{1,0:T(8,128)(2,1)S(1)} %collective-permute-done.4), channel_id=1, source_target_pairs={{0,2},{1,3},{2,0},{3,1},{4,6},{5,7},{6,4},{7,5},{8,10},{9,11},{10,... | collective-permute-start | bytes 153608 | tf_op jit(solution)/shard_map/ppermute | solution.py:33
  22.5 2.3 %collective-permute-start.7 = (bf16[40,640]{1,0:T(8,128)(2,1)S(1)}, bf16[40,640]{1,0:T(8,128)(2,1)S(1)}, u32[]{:S(2)}, u32[]{:S(2)}) collective-permute-start(bf16[40,640]{1,0:T(8,128)(2,1)S(1)} %collective-permute-done.4), channel_id=1, source_target_pairs={{0,1},{1,2},{2,3},{3,0},{4,5},{5,6},{6,7},{7,4},{8,9},{9,10},{10,1... | collective-permute-start | bytes 153608 | tf_op jit(solution)/shard_map/ppermute | solution.py:33
  24.9 4.6 %collective-permute-done.6 = bf16[40,640]{1,0:T(8,128)(2,1)S(1)} collective-permute-done((bf16[40,640]{1,0:T(8,128)(2,1)S(1)}, bf16[40,640]{1,0:T(8,128)(2,1)S(1)}, u32[]{:S(2)}, u32[]{:S(2)}) %collective-permute-start.6) | collective-permute-done | bytes 51232 | tf_op jit(solution)/shard_map/ppermute | solution.py:33
  29.6 1.9 %collective-permute-start.10 = (bf16[160,640]{1,0:T(8,128)(2,1)S(1)}, bf16[160,640]{1,0:T(8,128)(2,1)S(1)}, u32[]{:S(2)}, u32[]{:S(2)}) collective-permute-start(bf16[160,640]{1,0:T(8,128)(2,1)S(1)} %constant_dynamic-slice_fusion), channel_id=1, source_target_pairs={{0,128},{1,129},{2,130},{3,131},{4,132},{5,133},{6,134},{7,135},{8... | collective-permute-start | bytes 614408 | tf_op jit(solution)/shard_map/ppermute | solution.py:33
  31.5 8.3 %collective-permute-start.9 = (bf16[160,640]{1,0:T(8,128)(2,1)S(1)}, bf16[160,640]{1,0:T(8,128)(2,1)S(1)}, u32[]{:S(2)}, u32[]{:S(2)}) collective-permute-start(bf16[160,640]{1,0:T(8,128)(2,1)S(1)} %constant_dynamic-slice_fusion), channel_id=1, source_target_pairs={{0,256},{1,257},{2,258},{3,259},{4,260},{5,261},{6,262},{7,263},{8... | collective-permute-start | bytes 614408 | tf_op jit(solution)/shard_map/ppermute | solution.py:33
  39.8 1.9 %collective-permute-start.8 = (bf16[160,640]{1,0:T(8,128)(2,1)S(1)}, bf16[160,640]{1,0:T(8,128)(2,1)S(1)}, u32[]{:S(2)}, u32[]{:S(2)}) collective-permute-start(bf16[160,640]{1,0:T(8,128)(2,1)S(1)} %constant_dynamic-slice_fusion), channel_id=1, source_target_pairs={{0,384},{1,385},{2,386},{3,387},{4,388},{5,389},{6,390},{7,391},{8... | collective-permute-start | bytes 614408 | tf_op jit(solution)/shard_map/ppermute | solution.py:33
  41.8 1.2 %collective-permute-done.9 = bf16[160,640]{1,0:T(8,128)(2,1)S(1)} collective-permute-done((bf16[160,640]{1,0:T(8,128)(2,1)S(1)}, bf16[160,640]{1,0:T(8,128)(2,1)S(1)}, u32[]{:S(2)}, u32[]{:S(2)}) %collective-permute-start.9) | collective-permute-done | bytes 204832 | tf_op jit(solution)/shard_map/ppermute | solution.py:33
  43.0 5.7 %collective-permute-done.8 = bf16[160,640]{1,0:T(8,128)(2,1)S(1)} collective-permute-done((bf16[160,640]{1,0:T(8,128)(2,1)S(1)}, bf16[160,640]{1,0:T(8,128)(2,1)S(1)}, u32[]{:S(2)}, u32[]{:S(2)}) %collective-permute-start.8) | collective-permute-done | bytes 204832 | tf_op jit(solution)/shard_map/ppermute | solution.py:33
  48.7 0.1 pad_maximum_fusion.weight
  48.8 5.1 %collective-permute-start.11 = (bf16[640,640]{1,0:T(8,128)(2,1)S(1)}, bf16[640,640]{1,0:T(8,128)(2,1)S(1)}, u32[]{:S(2)}, u32[]{:S(2)}) collective-permute-start(bf16[640,640]{1,0:T(8,128)(2,1)S(1)} %pad_maximum_fusion.weight), channel_id=1, source_target_pairs={{0,4},{1,5},{2,6},{3,7},{4,0},{5,1},{6,2},{7,3},{8,12},{9,13},{10,... | collective-permute-start | bytes 2457608 | tf_op jit(solution)/shard_map/ppermute | solution.py:33
  53.9 3.2 %own.1 = (f32[640,256]{1,0:T(8,128)S(1)}, f32[16,256]{1,0:T(8,128)S(1)}, bf16[2,640,256]{2,1,0:T(8,128)(2,1)S(1)}) custom-call(bf16[16,32,640]{2,1,0:T(8,128)(2,1)S(1)} %copy-done.2, bf16[16,32,640]{2,1,0:T(8,128)(2,1)S(1)} %copy-done.1, bf16[16,32,640]{2,1,0:T(8,128)(2,1)S(1)} %copy-done), custom_call_target="tpu_custom_call" | custom-call | flops 1073741824 | bytes 4000000 | tf_op jit(solution)/shard_map/own/pallas_call | solution.py:238
  57.0 3.2 %edge.1 = (f32[640,256]{1,0:T(8,128)S(1)}, f32[16,256]{1,0:T(8,128)S(1)}, bf16[640,256]{1,0:T(8,128)(2,1)S(1)}) custom-call(bf16[16,32,640]{2,1,0:T(8,128)(2,1)S(1)} %copy-done.2, bf16[16,32,640]{2,1,0:T(8,128)(2,1)S(1)} %copy-done.1, bf16[32,16,640]{2,1,0:T(8,128)(2,1)S(1)} %collective-permute-done.left, bf16[2,640,256]{2,1,0:T(8,128)(2,1)S(1)} %get-tuple-element.11.values_t), custom_call_target="tpu_custom_call" | custom-call | flops 1073741824 | bytes 4000000 | tf_op jit(solution)/shard_map/edge/pallas_call | solution.py:242
  60.2 3.0 %lower_edge.1 = bf16[672,256]{1,0:T(8,128)(2,1)S(1)} custom-call(bf16[16,32,640]{2,1,0:T(8,128)(2,1)S(1)} %collective-permute-done.1.query, bf16[16,32,640]{2,1,0:T(8,128)(2,1)S(1)} %copy-done.1, bf16[32,16,640]{2,1,0:T(8,128)(2,1)S(1)} %collective-permute-done.left, bf16[2,640,256]{2,1,0:T(8,128)(2,1)S(1)} %get-tuple-element.11.values_t, ...), custom_call_target="tpu_custom_call" | custom-call | flops 1073741824 | bytes 4000000 | tf_op jit(solution)/shard_map/lower_edge/pallas_call | solution.py:250
  63.3 4.4 %collective-permute-start.2 = (bf16[672,256]{1,0:T(8,128)(2,1)S(1)}, bf16[672,256]{1,0:T(8,128)(2,1)S(1)}, u32[]{:S(2)}, u32[]{:S(2)}) collective-permute-start(bf16[672,256]{1,0:T(8,128)(2,1)S(1)} %lower_edge.1), channel_id=1, source_target_pairs={{0,4},{4,8},{8,12},{12,16},{16,20},{20,24},{24,28},{1,5},{5,9},{9,... | collective-permute-start | bytes 1032200 | tf_op jit(solution)/shard_map/ppermute | solution.py:43
  67.7 3.0 %lower_own.1 = bf16[672,256]{1,0:T(8,128)(2,1)S(1)} custom-call(bf16[16,32,640]{2,1,0:T(8,128)(2,1)S(1)} %collective-permute-done.1.query, bf16[16,32,640]{2,1,0:T(8,128)(2,1)S(1)} %copy-done.1, bf16[2,640,256]{2,1,0:T(8,128)(2,1)S(1)} %get-tuple-element.11.values_t), custom_call_target="tpu_custom_call" | custom-call | flops 1073741824 | bytes 4000000 | tf_op jit(solution)/shard_map/lower_own/pallas_call | solution.py:246
  70.7 2.4 %collective-permute-start.3 = (bf16[672,256]{1,0:T(8,128)(2,1)S(1)}, bf16[672,256]{1,0:T(8,128)(2,1)S(1)}, u32[]{:S(2)}, u32[]{:S(2)}) collective-permute-start(bf16[672,256]{1,0:T(8,128)(2,1)S(1)} %lower_own.1), channel_id=1, source_target_pairs={{0,4},{4,8},{8,12},{12,16},{16,20},{20,24},{24,28},{1,5},{5,9},{9,... | collective-permute-start | bytes 1032200 | tf_op jit(solution)/shard_map/ppermute | solution.py:43
  73.1 20.9 %collective-permute-done.2.upper_0 = bf16[672,256]{1,0:T(8,128)(2,1)S(1)} collective-permute-done((bf16[672,256]{1,0:T(8,128)(2,1)S(1)}, bf16[672,256]{1,0:T(8,128)(2,1)S(1)}, u32[]{:S(2)}, u32[]{:S(2)}) %collective-permute-start.2) | collective-permute-done | bytes 344096 | tf_op jit(solution)/shard_map/ppermute | solution.py:43
  94.0 3.7 %collective-permute-done.3.upper_1 = bf16[672,256]{1,0:T(8,128)(2,1)S(1)} collective-permute-done((bf16[672,256]{1,0:T(8,128)(2,1)S(1)}, bf16[672,256]{1,0:T(8,128)(2,1)S(1)}, u32[]{:S(2)}, u32[]{:S(2)}) %collective-permute-start.3) | collective-permute-done | bytes 344096 | tf_op jit(solution)/shard_map/ppermute | solution.py:43
  97.7 2.5 %project.1 = bf16[16,32,1280]{2,1,0:T(8,128)(2,1)} custom-call(f32[640,256]{1,0:T(8,128)S(1)} %get-tuple-element.12.mixed_0, f32[640,256]{1,0:T(8,128)S(1)} %get-tuple-element.13.mixed_1, f32[16,256]{1,0:T(8,128)S(1)} %get-tuple-element.14.stats_0, f32[16,256]{1,0:T(8,128)S(1)} %get-tuple-element.15.stats_1, ...), custom_call_target="tpu_custom_call" | custom-call | flops 838860800 | bytes 4000000 | tf_op jit(solution)/shard_map/project/pallas_call | solution.py:254
  (25 shorter events, 0.2 us)
Async XLA Ops:
  0.0 9.0 %slice-start = ((bf16[16,32,640]{2,1,0:T(8,128)(2,1)}), bf16[16,16,640]{2,1,0:T(8,128)(2,1)S(1)}, s32[]{:S(2)}) async-start(bf16[16,32,640]{2,1,0:T(8,128)(2,1)} %values.1), calls=%async_computation | async-start | bytes 655360 | tf_op jit(solution)/shard_map/slice | solution.py:227
  0.0 9.0 %slice-start.1 = ((bf16[16,32,640]{2,1,0:T(8,128)(2,1)}), bf16[16,16,640]{2,1,0:T(8,128)(2,1)S(1)}, s32[]{:S(2)}) async-start(bf16[16,32,640]{2,1,0:T(8,128)(2,1)} %keys.7), calls=%async_computation.1 | async-start | bytes 655360 | tf_op jit(solution)/shard_map/slice | solution.py:227
  0.0 12.3 %copy-start.2 = (bf16[16,32,640]{2,1,0:T(8,128)(2,1)S(1)}, bf16[16,32,640]{2,1,0:T(8,128)(2,1)}, u32[]{:S(2)}) copy-start(bf16[16,32,640]{2,1,0:T(8,128)(2,1)} %query.3) | copy-start | bytes 1966084
  0.0 15.5 %collective-permute-start.4 = (bf16[40,640]{1,0:T(8,128)(2,1)}, bf16[40,640]{1,0:T(8,128)(2,1)S(1)}, u32[]{:S(2)}, u32[]{:S(2)}) collective-permute-start(bf16[40,640]{1,0:T(8,128)(2,1)} %bitcast.1), channel_id=1, source_target_pairs={{0,0},{1,1},{2,2},{3,3},{4,4},{5,5},{6,6},{7,7},{8,8},{9,9},{10,10... | collective-permute-start | bytes 153608 | tf_op jit(solution)/shard_map/ppermute | solution.py:33
  9.1 48.0 %collective-permute-start = (bf16[32,16,640]{2,1,0:T(8,128)(2,1)S(1)}, bf16[32,16,640]{2,1,0:T(8,128)(2,1)S(1)}, u32[]{:S(2)}, u32[]{:S(2)}) collective-permute-start(bf16[32,16,640]{2,1,0:T(8,128)(2,1)S(1)} %pad_maximum_fusion.1), channel_id=1, source_target_pairs={{0,1},{1,2},{2,3},{4,5},{5,6},{6,7},{8,9},{9,10},{10,11},{12,13},{... | collective-permute-start | bytes 1966088 | tf_op jit(solution)/shard_map/ppermute | solution.py:43
  12.3 47.9 %collective-permute-start.1 = (bf16[16,32,640]{2,1,0:T(8,128)(2,1)S(1)}, bf16[16,32,640]{2,1,0:T(8,128)(2,1)S(1)}, u32[]{:S(2)}, u32[]{:S(2)}) collective-permute-start(bf16[16,32,640]{2,1,0:T(8,128)(2,1)S(1)} %copy-done.2), channel_id=1, source_target_pairs={{4,0},{8,4},{12,8},{16,12},{20,16},{24,20},{28,24},{5,1},{9,5},{13... | collective-permute-start | bytes 1966088 | tf_op jit(solution)/shard_map/ppermute | solution.py:43
  15.5 9.4 %collective-permute-start.5 = (bf16[40,640]{1,0:T(8,128)(2,1)S(1)}, bf16[40,640]{1,0:T(8,128)(2,1)S(1)}, u32[]{:S(2)}, u32[]{:S(2)}) collective-permute-start(bf16[40,640]{1,0:T(8,128)(2,1)S(1)} %collective-permute-done.4), channel_id=1, source_target_pairs={{0,3},{1,0},{2,1},{3,2},{4,7},{5,4},{6,5},{7,6},{8,11},{9,8},{10,9... | collective-permute-start | bytes 153608 | tf_op jit(solution)/shard_map/ppermute | solution.py:33
  19.9 34.0 %copy-start = (bf16[16,32,640]{2,1,0:T(8,128)(2,1)S(1)}, bf16[16,32,640]{2,1,0:T(8,128)(2,1)}, u32[]{:S(2)}) copy-start(bf16[16,32,640]{2,1,0:T(8,128)(2,1)} %values.1) | copy-start | bytes 1966084
  19.9 34.0 %copy-start.1 = (bf16[16,32,640]{2,1,0:T(8,128)(2,1)S(1)}, bf16[16,32,640]{2,1,0:T(8,128)(2,1)}, u32[]{:S(2)}) copy-start(bf16[16,32,640]{2,1,0:T(8,128)(2,1)} %keys.7) | copy-start | bytes 1966084
  19.9 9.6 %collective-permute-start.6 = (bf16[40,640]{1,0:T(8,128)(2,1)S(1)}, bf16[40,640]{1,0:T(8,128)(2,1)S(1)}, u32[]{:S(2)}, u32[]{:S(2)}) collective-permute-start(bf16[40,640]{1,0:T(8,128)(2,1)S(1)} %collective-permute-done.4), channel_id=1, source_target_pairs={{0,2},{1,3},{2,0},{3,1},{4,6},{5,7},{6,4},{7,5},{8,10},{9,11},{10,... | collective-permute-start | bytes 153608 | tf_op jit(solution)/shard_map/ppermute | solution.py:33
  22.5 7.0 %collective-permute-start.7 = (bf16[40,640]{1,0:T(8,128)(2,1)S(1)}, bf16[40,640]{1,0:T(8,128)(2,1)S(1)}, u32[]{:S(2)}, u32[]{:S(2)}) collective-permute-start(bf16[40,640]{1,0:T(8,128)(2,1)S(1)} %collective-permute-done.4), channel_id=1, source_target_pairs={{0,1},{1,2},{2,3},{3,0},{4,5},{5,6},{6,7},{7,4},{8,9},{9,10},{10,1... | collective-permute-start | bytes 153608 | tf_op jit(solution)/shard_map/ppermute | solution.py:33
  29.6 12.1 %collective-permute-start.10 = (bf16[160,640]{1,0:T(8,128)(2,1)S(1)}, bf16[160,640]{1,0:T(8,128)(2,1)S(1)}, u32[]{:S(2)}, u32[]{:S(2)}) collective-permute-start(bf16[160,640]{1,0:T(8,128)(2,1)S(1)} %constant_dynamic-slice_fusion), channel_id=1, source_target_pairs={{0,128},{1,129},{2,130},{3,131},{4,132},{5,133},{6,134},{7,135},{8... | collective-permute-start | bytes 614408 | tf_op jit(solution)/shard_map/ppermute | solution.py:33
  31.5 11.4 %collective-permute-start.9 = (bf16[160,640]{1,0:T(8,128)(2,1)S(1)}, bf16[160,640]{1,0:T(8,128)(2,1)S(1)}, u32[]{:S(2)}, u32[]{:S(2)}) collective-permute-start(bf16[160,640]{1,0:T(8,128)(2,1)S(1)} %constant_dynamic-slice_fusion), channel_id=1, source_target_pairs={{0,256},{1,257},{2,258},{3,259},{4,260},{5,261},{6,262},{7,263},{8... | collective-permute-start | bytes 614408 | tf_op jit(solution)/shard_map/ppermute | solution.py:33
  39.8 8.8 %collective-permute-start.8 = (bf16[160,640]{1,0:T(8,128)(2,1)S(1)}, bf16[160,640]{1,0:T(8,128)(2,1)S(1)}, u32[]{:S(2)}, u32[]{:S(2)}) collective-permute-start(bf16[160,640]{1,0:T(8,128)(2,1)S(1)} %constant_dynamic-slice_fusion), channel_id=1, source_target_pairs={{0,384},{1,385},{2,386},{3,387},{4,388},{5,389},{6,390},{7,391},{8... | collective-permute-start | bytes 614408 | tf_op jit(solution)/shard_map/ppermute | solution.py:33
  48.8 49.0 %collective-permute-start.11 = (bf16[640,640]{1,0:T(8,128)(2,1)S(1)}, bf16[640,640]{1,0:T(8,128)(2,1)S(1)}, u32[]{:S(2)}, u32[]{:S(2)}) collective-permute-start(bf16[640,640]{1,0:T(8,128)(2,1)S(1)} %pad_maximum_fusion.weight), channel_id=1, source_target_pairs={{0,4},{1,5},{2,6},{3,7},{4,0},{5,1},{6,2},{7,3},{8,12},{9,13},{10,... | collective-permute-start | bytes 2457608 | tf_op jit(solution)/shard_map/ppermute | solution.py:33
  63.3 30.8 %collective-permute-start.2 = (bf16[672,256]{1,0:T(8,128)(2,1)S(1)}, bf16[672,256]{1,0:T(8,128)(2,1)S(1)}, u32[]{:S(2)}, u32[]{:S(2)}) collective-permute-start(bf16[672,256]{1,0:T(8,128)(2,1)S(1)} %lower_edge.1), channel_id=1, source_target_pairs={{0,4},{4,8},{8,12},{12,16},{16,20},{20,24},{24,28},{1,5},{5,9},{9,... | collective-permute-start | bytes 1032200 | tf_op jit(solution)/shard_map/ppermute | solution.py:43
  70.7 27.0 %collective-permute-start.3 = (bf16[672,256]{1,0:T(8,128)(2,1)S(1)}, bf16[672,256]{1,0:T(8,128)(2,1)S(1)}, u32[]{:S(2)}, u32[]{:S(2)}) collective-permute-start(bf16[672,256]{1,0:T(8,128)(2,1)S(1)} %lower_own.1), channel_id=1, source_target_pairs={{0,4},{4,8},{8,12},{12,16},{16,20},{20,24},{24,28},{1,5},{5,9},{9,... | collective-permute-start | bytes 1032200 | tf_op jit(solution)/shard_map/ppermute | solution.py:43

commit v2 on v0

v2 whole, which is shorter than its diff:
```python
import functools
import math

import jax
import jax.numpy as jnp
from jax import lax
from jax.experimental import pallas as pl
from jax.experimental.pallas import tpu as pltpu
from jax.sharding import PartitionSpec as P

HEADS = 8
HDIM = 80
BLOCK = 16
TOKENS = BLOCK * BLOCK
CHANNELS = HEADS * HDIM
SCALE = math.log2(math.e) * HDIM ** (-0.5)
NEG = -1e30
PACKED = CHANNELS + 32
SIDE = 4
AXES = ("frame", "row", "col")


def place(x, zl, zh, core, y):
    return ((x * SIDE + zl) * 2 * SIDE + zh * 2 + core) * SIDE + y


def routed(block, members, target):
    route = []
    for x in range(SIDE):
        for zl in members:
            for zh in range(SIDE):
                for core in range(2):
                    for y in range(SIDE):
                        to = target(x, zh, core, y)
                        if to is not None:
                            route.append((place(x, zl, zh, core, y), place(to[0], zl, *to[1:])))
    return lax.ppermute(block, AXES, route)


def to_row(distance):
    def target(x, zh, core, y):
        row = zh * 2 + core + distance
        return (x, row // 2, row % 2, y) if 0 <= row < 2 * SIDE else None

    return target


def to_right(x, zh, core, y):
    return (x, zh, core, y + 1) if y + 1 < SIDE else None


def head_scores(keys, query_t, head):
    first = head * HDIM
    low = first // 128 * 128
    high = -(-(first + HDIM) // 128) * 128
    parts = []
    if first > low:
        parts.append(jnp.zeros((first - low, TOKENS), jnp.bfloat16))
    parts.append(query_t[first : first + HDIM])
    if high > first + HDIM:
        parts.append(jnp.zeros((high - first - HDIM, TOKENS), jnp.bfloat16))
    masked = jnp.concatenate(parts, axis=0)
    return jnp.dot(keys[:, low:high], masked, preferred_element_type=jnp.float32)


def attend(query_t, pair_a, pair_b, bias, emit):
    keys_a, keys_b = (p[:BLOCK].reshape(TOKENS, CHANNELS) for p in (pair_a, pair_b))
    values_a, values_b = (p[BLOCK:].reshape(TOKENS, CHANNELS).T for p in (pair_a, pair_b))
    for head in range(HEADS):
        rows = slice(head * HDIM, (head + 1) * HDIM)
        score_a = head_scores(keys_a, query_t, head)
        score_b = head_scores(keys_b, query_t, head)
        if bias is not None:
            score_a = score_a + bias
        largest = jnp.maximum(
            jnp.max(score_a, axis=0, keepdims=True), jnp.max(score_b, axis=0, keepdims=True)
        )
        largest = largest * SCALE
        weight_a = jnp.exp2(score_a * SCALE - largest)
        weight_b = jnp.exp2(score_b * SCALE - largest)
        total = jnp.sum(weight_a, axis=0, keepdims=True) + jnp.sum(weight_b, axis=0, keepdims=True)
        mixed = jnp.dot(
            values_a[rows], weight_a.astype(jnp.bfloat16), preferred_element_type=jnp.float32
        ) + jnp.dot(
            values_b[rows], weight_b.astype(jnp.bfloat16), preferred_element_type=jnp.float32
        )
        emit(head, rows, mixed, largest, total)


def block_of(ref, col):
    return ref[:, col * BLOCK : (col + 1) * BLOCK, :].reshape(TOKENS, CHANNELS)


def edge_bias(col):
    if col > 0:
        return None
    return jnp.where(lax.axis_index("col") > 0, jnp.float32(0.0), jnp.float32(NEG))


def pair_kernel(keys, values, pair_0, pair_1):
    for col, pair in ((0, pair_0), (1, pair_1)):
        pair[:BLOCK] = keys[:, col * BLOCK : (col + 1) * BLOCK]
        pair[BLOCK:] = values[:, col * BLOCK : (col + 1) * BLOCK]


def stack_kernel(*refs):
    for j, ref in enumerate(refs[:-1]):
        refs[-1][j] = ref[...]


def own_kernel(col, query, pair_a, pair_b, mixed_out, stats_out):
    def emit(head, rows, mixed, largest, total):
        mixed_out[rows] = mixed
        stats_out[head : head + 1] = largest
        stats_out[HEADS + head : HEADS + head + 1] = total

    attend(block_of(query, col).T, pair_a, pair_b, edge_bias(col), emit)


def part_kernel(col, query, pair_a, pair_b, packed, lse):
    def emit(head, rows, mixed, largest, total):
        packed[rows] = (mixed * (1.0 / total)).astype(jnp.bfloat16)
        lse[head : head + 1] = largest + jnp.log2(total)

    attend(block_of(query, col).T, pair_a, pair_b, edge_bias(col), emit)
    whole = lse[...]
    high = whole.astype(jnp.bfloat16).astype(jnp.float32)
    middle = (whole - high).astype(jnp.bfloat16).astype(jnp.float32)
    low = whole - high - middle
    packed[CHANNELS : CHANNELS + 16] = jnp.concatenate([high, middle], axis=0).astype(jnp.bfloat16)
    packed[CHANNELS + 16 : CHANNELS + 32] = jnp.concatenate(
        [low, jnp.zeros_like(whole)], axis=0
    ).astype(jnp.bfloat16)


def order_kernel(weight, other, full):
    row = lax.axis_index("row")
    z_hi, core = row // 2, row % 2
    span = full.shape[0] // (2 * SIDE)
    for item in range(SIDE):
        holder = lax.rem(z_hi + item, SIDE) * 2
        for source, which in ((weight, core), (other, 1 - core)):
            start = pl.multiple_of((holder + which) * span, span)
            full[pl.ds(start, span)] = source[item * span : (item + 1) * span]


def project_kernel(mixed, stats, upper, full, *refs):
    projected, merged = refs[-2:]
    largest, total = stats[:HEADS], stats[HEADS:]
    parts = upper[CHANNELS : CHANNELS + 32].astype(jnp.float32)
    lse = parts[:HEADS] + parts[HEADS : 2 * HEADS] + parts[2 * HEADS : 3 * HEADS]
    lse = jnp.where(lax.axis_index("row") > 0, lse, jnp.float32(NEG))
    top = jnp.maximum(largest, lse)
    own_w = jnp.exp2(largest - top)
    upper_w = jnp.exp2(lse - top)
    share = 1.0 / (total * own_w + upper_w)
    own_w, upper_w = own_w * share, upper_w * share
    for head in range(HEADS):
        rows = slice(head * HDIM, (head + 1) * HDIM)
        merged[rows] = (
            mixed[rows] * own_w[head : head + 1]
            + upper[rows].astype(jnp.float32) * upper_w[head : head + 1]
        ).astype(jnp.bfloat16)
    result = lax.dot_general(
        merged[...].T, full[...], (((1,), (1,)), ((), ())), preferred_element_type=jnp.float32
    )
    projected[...] = result.astype(jnp.bfloat16).reshape(projected.shape)


def call(kernel, outs, scratch=(), flops=0, name=None, **more):
    return pl.pallas_call(
        kernel,
        out_shape=outs,
        scratch_shapes=list(scratch),
        compiler_params=pltpu.CompilerParams(vmem_limit_bytes=32 * 1024 * 1024),
        cost_estimate=pl.CostEstimate(flops=flops, bytes_accessed=1024, transcendentals=0),
        name=name,
        **more,
    )


STACK_FLOPS = 6_000_000_000
OWN_FLOPS = 1024
PAIR_FLOPS = 1024
PART_FLOPS = 1024


def own_part(col, query, pair_a, pair_b):
    return call(
        functools.partial(own_kernel, col),
        (
            jax.ShapeDtypeStruct((CHANNELS, TOKENS), jnp.float32),
            jax.ShapeDtypeStruct((2 * HEADS, TOKENS), jnp.float32),
        ),
        flops=OWN_FLOPS if col else 1024, name=f"own_{col}",
    )(query, pair_a, pair_b)


def upper_part(col, query, pair_a, pair_b, *earlier):
    def kernel(query, pair_a, pair_b, *refs):
        part_kernel(col, query, pair_a, pair_b, *refs[-2:])

    whole = pl.BlockSpec(memory_space=pltpu.VMEM)
    return call(
        kernel,
        jax.ShapeDtypeStruct((PACKED, TOKENS), jnp.bfloat16),
        (pltpu.VMEM((HEADS, TOKENS), jnp.float32),),
        flops=PART_FLOPS, name=f"part_{col}",
        in_specs=[whole] * 3 + [pl.BlockSpec(memory_space=pl.ANY)] * len(earlier),
    )(query, pair_a, pair_b, *earlier)


def project(col, own, upper, full, shape, before=None):
    whole = lambda a: pl.BlockSpec(a.shape, lambda i: (0,) * a.ndim)
    operands = [*own, upper, full]
    specs = [whole(a) for a in operands]
    aliases = {}
    if before is not None:
        aliases = {len(operands): 0}
        operands.append(before)
        specs.append(pl.BlockSpec(memory_space=pl.ANY))
    return call(
        project_kernel,
        jax.ShapeDtypeStruct(shape, jnp.bfloat16),
        (pltpu.VMEM((CHANNELS, TOKENS), jnp.bfloat16),),
        flops=1024, name=f"project_{col}",
        grid=(1,), in_specs=specs,
        out_specs=pl.BlockSpec((BLOCK, BLOCK, shape[2]), lambda i: (0, col, 0)),
        input_output_aliases=aliases,
    )(*operands)


def from_part(block, distance):
    return routed(
        block, range(SIDE), lambda x, zh, c, y: (x, (zh - distance) % SIDE, c, y)
    )


def weight_both(half, members):
    other = routed(half, members, lambda x, zh, c, y: (x, zh, 1 - c, y))
    return call(
        order_kernel, jax.ShapeDtypeStruct((2 * half.shape[0], half.shape[1]), half.dtype), name="order"
    )(half, other)


def after(value, *others):
    return lax.optimization_barrier((value, *others))[0]


def outputs(own_1, own_0, upper_1, upper_0, full, query):
    shape = (query.shape[0], query.shape[1], full.shape[0])
    right = project(1, own_1, upper_1, full, shape)
    return project(0, own_0, upper_0, full, shape, right)


def by_frame(late, early, *operands):
    z_lo = lax.rem(lax.axis_index("frame"), SIDE)
    half = SIDE // 2
    return lax.cond(
        z_lo < half,
        functools.partial(late, range(half)),
        functools.partial(early, range(half, SIDE)),
        *operands,
    )


def on_device(query, keys, values, out_weight):
    frames = range(SIDE)
    shard = out_weight.T
    following = from_part(shard, 1)
    previous = from_part(shard, -1)
    lower_query = routed(query, frames, to_row(-1))
    pair_0, pair_1 = call(
        pair_kernel,
        [jax.ShapeDtypeStruct((2 * BLOCK, BLOCK, CHANNELS), jnp.bfloat16)] * 2,
        flops=PAIR_FLOPS, name="pair",
    )(keys, values)
    left = routed(pair_1, frames, to_right)
    own_1 = own_part(1, query, pair_0, pair_1)
    previous = after(previous, following, own_1[1])
    far = from_part(previous, -1)
    items = call(
        stack_kernel, jax.ShapeDtypeStruct((SIDE, *shard.shape), shard.dtype),
        flops=STACK_FLOPS, name="stack",
    )(shard, following, far, previous)

    def gather(items):
        half = lax.all_gather(items, "col", axis=1, tiled=True)
        return half.reshape(-1, half.shape[2])

    def first_late(members, items):
        return gather(items)

    def first_early(members, items):
        return jnp.zeros((SIDE * SIDE * items.shape[1], CHANNELS), items.dtype)

    half = by_frame(first_late, first_early, items)
    part_1 = upper_part(1, lower_query, pair_0, pair_1, half)
    upper_1 = routed(part_1, frames, to_row(1))
    part_0 = upper_part(0, lower_query, left, pair_0, part_1)
    upper_0 = routed(part_0, frames, to_row(1))

    def last_late(members, items, half, query, left, pair_0):
        return weight_both(half, members), *own_part(0, query, left, pair_0)

    def last_early(members, items, half, query, left, pair_0):
        own_0 = own_part(0, query, left, pair_0)
        return weight_both(gather(after(items, own_0[1])), members), *own_0

    full, *own_0 = by_frame(
        last_late, last_early, after(items, part_0), half, query, left, pair_0
    )
    return outputs(own_1, own_0, upper_1, upper_0, full, query)


def solution(mesh):
    placed = (
        P(("frame", "row"), "col", None),
        P(("frame", "row"), "col", None),
        P(("frame", "row"), "col", None),
        P(None, ("row", "col")),
    )
    return jax.shard_map(
        on_device,
        mesh=mesh,
        in_specs=placed,
        out_specs=P(("frame", "row"), "col", None),
        check_vma=False,
    )
```

time: 168 us -> 81.2 us (0.48)
  waiting for transfers between devices: 58.5 us -> 6.35 us
  local copies, waits for them, and re-layouts: 34.9 us -> 2.19 us
  matrix products: 19.1 us -> 0 us
  Pallas kernels: 0 us -> 18 us
  starting transfers between devices: 26.3 us -> 40.1 us
  between operations: 13.5 us -> 0.17 us
  blocking collectives: 0 us -> 12.9 us
  other arithmetic: 9.31 us -> 0 us
  loops' own time: 5.2 us -> 0.29 us
    all_gather x1 -> x0, waiting for transfers between devices: 45.6 us -> none  [on_device(): lax.all_gather(out_weight, ('row', 'col'), axis=1, tiled=True)]
    dot_general x5 -> x0, matrix products: 19.1 us -> none  [the longest x2 11.1 us: attend_block(): jnp.einsum('hqk,khd->qhd', rounded, v_heads, preferred_element_type=jnp.f...]
    pallas_call x0 -> x9, Pallas kernels: none -> 18 us  [the longest x2 7.41 us: own_part(): call(functools.partial(own_kernel, col), (jax.ShapeDtypeStruct((CHANNELS,...]
    reshape x6 -> x0, local copies, waits for them, and re-layouts: 16.3 us -> none  [the longest x2 7.37 us: attend_block(): k_heads = key_block.reshape(4 * side * side, HEADS, HDIM)]
    ppermute x6 -> x8, starting transfers between devices: 26.3 us -> 40.1 us  [routed(): return lax.ppermute(block, AXES, route)]
    all_gather x0 -> x1, blocking collectives: none -> 12.9 us  [gather(): half = lax.all_gather(items, 'col', axis=1, tiled=True)]
    dynamic_slice x6 -> x0, local copies, waits for them, and re-layouts: 10.8 us -> none  [the longest x2 6.08 us: one_block(): lax.dynamic_slice(ext_k, (brow * BLOCK, bcol * BLOCK, zero), (2 * BLOCK,...]
    ppermute x6 -> x8, waiting for transfers between devices: 12.9 us -> 6.35 us  [routed(): return lax.ppermute(block, AXES, route)]
  transfers between devices with their start and end apart: 7 -> 8, of which waited for: 5 -> 2; matrix products, arithmetic and copies ran while one was open for 33% -> 0% of each run, Pallas kernels for 0% -> 20%
where the time goes in v2:
time: 81.2 us; the launch traced here: 80.1 us
  starting transfers between devices  40.1 us (49%)
  Pallas kernels  18 us (22%)
  blocking collectives  12.9 us (16%)
  waiting for transfers between devices  6.35 us (8%)
  local copies, waits for them, and re-layouts  2.19 us (3%)
    ppermute x8, starting transfers between devices, routed(): return lax.ppermute(block, AXES, route)  40.1 us
    all_gather x1, blocking collectives, gather(): half = lax.all_gather(items, 'col', axis=1, tiled=True)  12.9 us
    pallas_call x2, Pallas kernels, own_part(): call(functools.partial(own_kernel, col), (jax.ShapeDtypeStruct((CHANNELS,...  7.41 us
    pallas_call x2, Pallas kernels, upper_part(): call(kernel, jax.ShapeDtypeStruct((PACKED, TOKENS), jnp.bfloat16), (pltpu...  7.13 us
    ppermute x8, waiting for transfers between devices, routed(): return lax.ppermute(block, AXES, route)  6.35 us
    pallas_call x2, Pallas kernels, project(): call(project_kernel, jax.ShapeDtypeStruct(shape, jnp.bfloat16), (pltpu.VM...  3.19 us
    unnamed x12, local copies, waits for them, and re-layouts  2.19 us
  transfers between devices with their start and end apart: 8, of which 2 were waited for; matrix products, arithmetic and copies ran while one was open for 0% of the time, Pallas kernels for 20%

profile of v2, /device:TPU:1, one launch (start us, length us, event | category | flops | bytes accessed | tf_op | source)
XLA Modules:
  0.0 80.1 jit_solution(13192443360033532659)
XLA Ops:
  0.0 9.6 %collective-permute-start.4 = (bf16[40,640]{1,0:T(8,128)(2,1)}, bf16[40,640]{1,0:T(8,128)(2,1)S(1)}, u32[]{:S(2)}, u32[]{:S(2)}) collective-permute-start(bf16[40,640]{1,0:T(8,128)(2,1)} %bitcast.5), channel_id=1, source_target_pairs={{0,8},{1,9},{2,10},{3,11},{4,12},{5,13},{6,14},{7,15},{8,16},{9,17... | collective-permute-start | bytes 153608 | tf_op jit(solution)/shard_map/ppermute | solution.py:37
  9.6 5.6 %collective-permute-start.3 = (bf16[40,640]{1,0:T(8,128)(2,1)}, bf16[40,640]{1,0:T(8,128)(2,1)S(1)}, u32[]{:S(2)}, u32[]{:S(2)}) collective-permute-start(bf16[40,640]{1,0:T(8,128)(2,1)} %bitcast.6), channel_id=1, source_target_pairs={{0,24},{1,25},{2,26},{3,27},{4,28},{5,29},{6,30},{7,31},{8,0},{9,1... | collective-permute-start | bytes 153608 | tf_op jit(solution)/shard_map/ppermute | solution.py:37
  15.2 3.3 %collective-permute-start.6 = (bf16[16,32,640]{2,1,0:T(8,128)(2,1)}, bf16[16,32,640]{2,1,0:T(8,128)(2,1)S(1)}, u32[]{:S(2)}, u32[]{:S(2)}) collective-permute-start(bf16[16,32,640]{2,1,0:T(8,128)(2,1)} %query.1), channel_id=1, source_target_pairs={{4,0},{5,1},{6,2},{7,3},{8,4},{9,5},{10,6},{11,7},{12,8},{13,9},{1... | collective-permute-start | bytes 1966088 | tf_op jit(solution)/shard_map/ppermute | solution.py:37
  18.6 1.1 %copy-done = bf16[16,32,640]{2,1,0:T(8,128)(2,1)S(1)} copy-done((bf16[16,32,640]{2,1,0:T(8,128)(2,1)S(1)}, bf16[16,32,640]{2,1,0:T(8,128)(2,1)}, u32[]{:S(2)}) %copy-start) | copy-done | bytes 655384
  19.6 1.1 %copy-done.1 = bf16[16,32,640]{2,1,0:T(8,128)(2,1)S(1)} copy-done((bf16[16,32,640]{2,1,0:T(8,128)(2,1)S(1)}, bf16[16,32,640]{2,1,0:T(8,128)(2,1)}, u32[]{:S(2)}) %copy-start.1) | copy-done | bytes 655384
  20.7 0.1 pair.1
  20.8 3.8 %collective-permute-start.2 = (bf16[32,16,640]{2,1,0:T(8,128)(2,1)S(1)}, bf16[32,16,640]{2,1,0:T(8,128)(2,1)}, u32[]{:S(2)}, u32[]{:S(2)}) collective-permute-start(bf16[32,16,640]{2,1,0:T(8,128)(2,1)S(1)} %get-tuple-element.47.pair_b), channel_id=1, source_target_pairs={{0,1},{1,2},{2,3},{4,5},{5,6},{6,7},{8,9},{9,10},{10,11},{12,13},{... | collective-permute-start | bytes 1966088 | tf_op jit(solution)/shard_map/ppermute | solution.py:37
  24.6 3.2 %own_1.1 = (f32[640,256]{1,0:T(8,128)S(1)}, f32[16,256]{1,0:T(8,128)S(1)}) custom-call(bf16[16,32,640]{2,1,0:T(8,128)(2,1)S(1)} %copy-done.4, bf16[32,16,640]{2,1,0:T(8,128)(2,1)S(1)} %get-tuple-element.48.pair_a.pair_b, bf16[32,16,640]{2,1,0:T(8,128)(2,1)S(1)} %get-tuple-element.47.pair_b), custom_call_target="tpu_custom_call" | custom-call | flops 1024 | bytes 1024 | tf_op jit(solution)/shard_map/own_1/pallas_call | solution.py:189
  27.8 5.2 %collective-permute-start.5 = (bf16[40,640]{1,0:T(8,128)(2,1)S(1)}, bf16[40,640]{1,0:T(8,128)(2,1)S(1)}, u32[]{:S(2)}, u32[]{:S(2)}) collective-permute-start(bf16[40,640]{1,0:T(8,128)(2,1)S(1)} %collective-permute-done.4.refs_3_), channel_id=1, source_target_pairs={{0,8},{1,9},{2,10},{3,11},{4,12},{5,13},{6,14},{7,15},{8,16},{9,17... | collective-permute-start | bytes 153608 | tf_op jit(solution)/shard_map/ppermute | solution.py:37
  33.0 4.2 %collective-permute-done.5.refs_2_ = bf16[40,640]{1,0:T(8,128)(2,1)S(1)} collective-permute-done((bf16[40,640]{1,0:T(8,128)(2,1)S(1)}, bf16[40,640]{1,0:T(8,128)(2,1)S(1)}, u32[]{:S(2)}, u32[]{:S(2)}) %collective-permute-start.5) | collective-permute-done | bytes 51232 | tf_op jit(solution)/shard_map/ppermute | solution.py:37
  37.2 13.0 %conditional.2 = (bf16[640,640]{1,0:T(8,128)(2,1)}) conditional(s32[]{:T(128)} %convert_element_type.4, () %tuple.23, bf16[4,40,640]{2,1,0:T(8,128)(2,1)S(1)} %stack.1), branch_computations={%region_0.0_spmd, %region_1.0_spmd} | conditional | bytes 1024008 | solution.py:259
  37.2 12.9 %all_gather.4 = bf16[4,160,640]{2,1,0:T(8,128)(2,1)} all-gather(bf16[4,40,640]{2,1,0:T(8,128)(2,1)S(1)} %param.1), channel_id=1, replica_groups=mesh['frame'=16,'row'=8,'col'=4] {'col'}, dimensions={1}, use_global_device_ids=true | all-gather | bytes 1024000 | tf_op jit(solution)/shard_map/cond/branch_1_fun/all_gather | solution.py:288
  50.2 2.1 %collective-permute-done.6.query = bf16[16,32,640]{2,1,0:T(8,128)(2,1)S(1)} collective-permute-done((bf16[16,32,640]{2,1,0:T(8,128)(2,1)}, bf16[16,32,640]{2,1,0:T(8,128)(2,1)S(1)}, u32[]{:S(2)}, u32[]{:S(2)}) %collective-permute-start.6) | collective-permute-done | bytes 655392 | tf_op jit(solution)/shard_map/ppermute | solution.py:37
  52.3 3.0 %part_1.1.refs_0_ = bf16[672,256]{1,0:T(8,128)(2,1)S(1)} custom-call(bf16[16,32,640]{2,1,0:T(8,128)(2,1)S(1)} %collective-permute-done.6.query, bf16[32,16,640]{2,1,0:T(8,128)(2,1)S(1)} %get-tuple-element.48.pair_a.pair_b, bf16[32,16,640]{2,1,0:T(8,128)(2,1)S(1)} %get-tuple-element.47.pair_b, bf16[640,640]{1,0:T(8,128)(2,1)} %get-tuple-element.62.refs_0_), custom_call_target="tpu_custom_call" | custom-call | flops 1024 | bytes 1024 | tf_op jit(solution)/shard_map/part_1/pallas_call | solution.py:204
  55.3 0.0 copy-start.5
  55.3 8.1 %collective-permute-start.8 = (bf16[672,256]{1,0:T(8,128)(2,1)S(1)}, bf16[672,256]{1,0:T(8,128)(2,1)S(1)}, u32[]{:S(2)}, u32[]{:S(2)}) collective-permute-start(bf16[672,256]{1,0:T(8,128)(2,1)S(1)} %part_1.1.refs_0_), channel_id=1, source_target_pairs={{0,4},{1,5},{2,6},{3,7},{4,8},{5,9},{6,10},{7,11},{8,12},{9,13},{1... | collective-permute-start | bytes 1032200 | tf_op jit(solution)/shard_map/ppermute | solution.py:37
  63.5 4.1 %part_0.1 = bf16[672,256]{1,0:T(8,128)(2,1)S(1)} custom-call(bf16[16,32,640]{2,1,0:T(8,128)(2,1)S(1)} %collective-permute-done.6.query, bf16[32,16,640]{2,1,0:T(8,128)(2,1)} %collective-permute-done.2.pair_a, bf16[32,16,640]{2,1,0:T(8,128)(2,1)S(1)} %get-tuple-element.48.pair_a.pair_b, bf16[672,256]{1,0:T(8,128)(2,1)S(1)} %part_1.1.refs_0_), custom_call_target="tpu_custom_call" | custom-call | flops 1024 | bytes 1024 | tf_op jit(solution)/shard_map/part_0/pallas_call | solution.py:204
  67.6 1.9 %collective-permute-start.7 = (bf16[672,256]{1,0:T(8,128)(2,1)S(1)}, bf16[672,256]{1,0:T(8,128)(2,1)S(1)}, u32[]{:S(2)}, u32[]{:S(2)}) collective-permute-start(bf16[672,256]{1,0:T(8,128)(2,1)S(1)} %part_0.1), channel_id=1, source_target_pairs={{0,4},{1,5},{2,6},{3,7},{4,8},{5,9},{6,10},{7,11},{8,12},{9,13},{1... | collective-permute-start | bytes 1032200 | tf_op jit(solution)/shard_map/ppermute | solution.py:37
  69.5 7.3 %conditional.3 = (bf16[1280,640]{1,0:T(8,128)(2,1)S(1)}, f32[640,256]{1,0:T(8,128)S(1)}, f32[16,256]{1,0:T(8,128)S(1)}) conditional(s32[]{:T(128)} %convert_element_type.4, (bf16[16,32,640]{2,1,0:T(8,128)(2,1)S(1)}, bf16[32,16,640]{2,1,0:T(8,128)(2,1)}, bf16[32,16,640]{2,1,0:T(8,128)(2,1)S(1)}, bf16[4,40,640]{2,1,0:T(8,128)(2,1)S(1)}) %tuple.32, ...), branch_computations={%region_2.0_spmd, %region_3.0_spmd} | conditional | flops 1024 | bytes 4302912 | solution.py:259
  69.6 2.6 %collective-permute-start.1 = (bf16[640,640]{1,0:T(8,128)(2,1)S(1)}, bf16[640,640]{1,0:T(8,128)(2,1)S(1)}, u32[]{:S(2)}, u32[]{:S(2)}) collective-permute-start(bf16[640,640]{1,0:T(8,128)(2,1)S(1)} %get-tuple-element.32.weight), channel_id=1, source_target_pairs={{0,4},{1,5},{2,6},{3,7},{4,0},{5,1},{6,2},{7,3},{8,12},{9,13},{10,... | collective-permute-start | bytes 2457608 | tf_op jit(solution)/shard_map/cond/branch_1_fun/ppermute | solution.py:37
  72.2 4.3 %own_0.3 = (f32[640,256]{1,0:T(8,128)S(1)}, f32[16,256]{1,0:T(8,128)S(1)}) custom-call(bf16[16,32,640]{2,1,0:T(8,128)(2,1)S(1)} %get-tuple-element.33.query, bf16[32,16,640]{2,1,0:T(8,128)(2,1)} %get-tuple-element.34.pair_a, bf16[32,16,640]{2,1,0:T(8,128)(2,1)S(1)} %get-tuple-element.35.pair_b), custom_call_target="tpu_custom_call" | custom-call | flops 1024 | bytes 1024 | tf_op jit(solution)/shard_map/cond/branch_1_fun/own_0/pallas_call | solution.py:189
  76.5 0.2 order.3
  76.9 1.6 %project_1.1.refs_0_ = bf16[16,32,1280]{2,1,0:T(8,128)(2,1)} custom-call(f32[640,256]{1,0:T(8,128)S(1)} %get-tuple-element.55.mixed, f32[16,256]{1,0:T(8,128)S(1)} %get-tuple-element.49.stats, bf16[672,256]{1,0:T(8,128)(2,1)S(1)} %collective-permute-done.8.upper, bf16[1280,640]{1,0:T(8,128)(2,1)S(1)} %get-tuple-element.54.full), custom_call_target="tpu_custom_call" | custom-call | flops 1024 | bytes 1024 | tf_op jit(solution)/shard_map/project_1/pallas_call | solution.py:222
  78.5 1.6 %project_0.1 = bf16[16,32,1280]{2,1,0:T(8,128)(2,1)} custom-call(f32[640,256]{1,0:T(8,128)S(1)} %get-tuple-element.52.mixed, f32[16,256]{1,0:T(8,128)S(1)} %get-tuple-element.53.stats, bf16[672,256]{1,0:T(8,128)(2,1)S(1)} %collective-permute-done.7.upper, bf16[1280,640]{1,0:T(8,128)(2,1)S(1)} %get-tuple-element.54.full, ...), custom_call_target="tpu_custom_call", output_to_operand_aliasing={{}: (4, {})} | custom-call | flops 1024 | bytes 1024 | tf_op jit(solution)/shard_map/project_0/pallas_call | solution.py:222
  (16 shorter events, 0.0 us)
Async XLA Ops:
  0.0 27.8 %collective-permute-start.4 = (bf16[40,640]{1,0:T(8,128)(2,1)}, bf16[40,640]{1,0:T(8,128)(2,1)S(1)}, u32[]{:S(2)}, u32[]{:S(2)}) collective-permute-start(bf16[40,640]{1,0:T(8,128)(2,1)} %bitcast.5), channel_id=1, source_target_pairs={{0,8},{1,9},{2,10},{3,11},{4,12},{5,13},{6,14},{7,15},{8,16},{9,17... | collective-permute-start | bytes 153608 | tf_op jit(solution)/shard_map/ppermute | solution.py:37
  9.6 18.1 %collective-permute-start.3 = (bf16[40,640]{1,0:T(8,128)(2,1)}, bf16[40,640]{1,0:T(8,128)(2,1)S(1)}, u32[]{:S(2)}, u32[]{:S(2)}) collective-permute-start(bf16[40,640]{1,0:T(8,128)(2,1)} %bitcast.6), channel_id=1, source_target_pairs={{0,24},{1,25},{2,26},{3,27},{4,28},{5,29},{6,30},{7,31},{8,0},{9,1... | collective-permute-start | bytes 153608 | tf_op jit(solution)/shard_map/ppermute | solution.py:37
  15.2 37.1 %collective-permute-start.6 = (bf16[16,32,640]{2,1,0:T(8,128)(2,1)}, bf16[16,32,640]{2,1,0:T(8,128)(2,1)S(1)}, u32[]{:S(2)}, u32[]{:S(2)}) collective-permute-start(bf16[16,32,640]{2,1,0:T(8,128)(2,1)} %query.1), channel_id=1, source_target_pairs={{4,0},{5,1},{6,2},{7,3},{8,4},{9,5},{10,6},{11,7},{12,8},{13,9},{1... | collective-permute-start | bytes 1966088 | tf_op jit(solution)/shard_map/ppermute | solution.py:37
  18.6 1.1 %copy-start = (bf16[16,32,640]{2,1,0:T(8,128)(2,1)S(1)}, bf16[16,32,640]{2,1,0:T(8,128)(2,1)}, u32[]{:S(2)}) copy-start(bf16[16,32,640]{2,1,0:T(8,128)(2,1)} %keys.1) | copy-start | bytes 1966084
  19.6 1.1 %copy-start.1 = (bf16[16,32,640]{2,1,0:T(8,128)(2,1)S(1)}, bf16[16,32,640]{2,1,0:T(8,128)(2,1)}, u32[]{:S(2)}) copy-start(bf16[16,32,640]{2,1,0:T(8,128)(2,1)} %values.1) | copy-start | bytes 1966084
  20.7 3.9 %copy-start.4 = (bf16[16,32,640]{2,1,0:T(8,128)(2,1)S(1)}, bf16[16,32,640]{2,1,0:T(8,128)(2,1)}, u32[]{:S(2)}) copy-start(bf16[16,32,640]{2,1,0:T(8,128)(2,1)} %query.1) | copy-start | bytes 1966084
  20.7 16.4 %copy-start.2 = (bf16[640,40]{0,1:T(8,128)(2,1)S(1)}, bf16[640,40]{0,1:T(8,128)(2,1)}, u32[]{:S(2)}) copy-start(bf16[640,40]{0,1:T(8,128)(2,1)} %param.11) | copy-start | bytes 153604
  20.8 42.6 %collective-permute-start.2 = (bf16[32,16,640]{2,1,0:T(8,128)(2,1)S(1)}, bf16[32,16,640]{2,1,0:T(8,128)(2,1)}, u32[]{:S(2)}, u32[]{:S(2)}) collective-permute-start(bf16[32,16,640]{2,1,0:T(8,128)(2,1)S(1)} %get-tuple-element.47.pair_b), channel_id=1, source_target_pairs={{0,1},{1,2},{2,3},{4,5},{5,6},{6,7},{8,9},{9,10},{10,11},{12,13},{... | collective-permute-start | bytes 1966088 | tf_op jit(solution)/shard_map/ppermute | solution.py:37
  27.8 9.4 %collective-permute-start.5 = (bf16[40,640]{1,0:T(8,128)(2,1)S(1)}, bf16[40,640]{1,0:T(8,128)(2,1)S(1)}, u32[]{:S(2)}, u32[]{:S(2)}) collective-permute-start(bf16[40,640]{1,0:T(8,128)(2,1)S(1)} %collective-permute-done.4.refs_3_), channel_id=1, source_target_pairs={{0,8},{1,9},{2,10},{3,11},{4,12},{5,13},{6,14},{7,15},{8,16},{9,17... | collective-permute-start | bytes 153608 | tf_op jit(solution)/shard_map/ppermute | solution.py:37
  55.3 14.2 %copy-start.3 = (bf16[640,640]{1,0:T(8,128)(2,1)S(1)}, bf16[640,640]{1,0:T(8,128)(2,1)}, u32[]{:S(2)}) copy-start(bf16[640,640]{1,0:T(8,128)(2,1)} %get-tuple-element.62.refs_0_) | copy-start | bytes 2457604
  55.3 14.2 %copy-start.5 = (bf16[16,32,640]{2,1,0:T(8,128)(2,1)S(1)}, bf16[16,32,640]{2,1,0:T(8,128)(2,1)}, u32[]{:S(2)}) copy-start(bf16[16,32,640]{2,1,0:T(8,128)(2,1)} %query.1) | copy-start | bytes 1966084
  55.3 21.5 %collective-permute-start.8 = (bf16[672,256]{1,0:T(8,128)(2,1)S(1)}, bf16[672,256]{1,0:T(8,128)(2,1)S(1)}, u32[]{:S(2)}, u32[]{:S(2)}) collective-permute-start(bf16[672,256]{1,0:T(8,128)(2,1)S(1)} %part_1.1.refs_0_), channel_id=1, source_target_pairs={{0,4},{1,5},{2,6},{3,7},{4,8},{5,9},{6,10},{7,11},{8,12},{9,13},{1... | collective-permute-start | bytes 1032200 | tf_op jit(solution)/shard_map/ppermute | solution.py:37
  67.6 10.9 %collective-permute-start.7 = (bf16[672,256]{1,0:T(8,128)(2,1)S(1)}, bf16[672,256]{1,0:T(8,128)(2,1)S(1)}, u32[]{:S(2)}, u32[]{:S(2)}) collective-permute-start(bf16[672,256]{1,0:T(8,128)(2,1)S(1)} %part_0.1), channel_id=1, source_target_pairs={{0,4},{1,5},{2,6},{3,7},{4,8},{5,9},{6,10},{7,11},{8,12},{9,13},{1... | collective-permute-start | bytes 1032200 | tf_op jit(solution)/shard_map/ppermute | solution.py:37
  69.6 6.9 %collective-permute-start.1 = (bf16[640,640]{1,0:T(8,128)(2,1)S(1)}, bf16[640,640]{1,0:T(8,128)(2,1)S(1)}, u32[]{:S(2)}, u32[]{:S(2)}) collective-permute-start(bf16[640,640]{1,0:T(8,128)(2,1)S(1)} %get-tuple-element.32.weight), channel_id=1, source_target_pairs={{0,4},{1,5},{2,6},{3,7},{4,0},{5,1},{6,2},{7,3},{8,12},{9,13},{10,... | collective-permute-start | bytes 2457608 | tf_op jit(solution)/shard_map/cond/branch_1_fun/ppermute | solution.py:37

commit v3 on v2

--- a/solution.py
+++ b/solution.py
@@ -276,13 +276,13 @@
         flops=PAIR_FLOPS, name="pair",
     )(keys, values)
     left = routed(pair_1, frames, to_right)
+    previous = after(previous, following, pair_1)
+    far = from_part(previous, -1)
     own_1 = own_part(1, query, pair_0, pair_1)
-    previous = after(previous, following, own_1[1])
-    far = from_part(previous, -1)
     items = call(
         stack_kernel, jax.ShapeDtypeStruct((SIDE, *shard.shape), shard.dtype),
         flops=STACK_FLOPS, name="stack",
-    )(shard, following, far, previous)
+    )(shard, following, after(far, own_1[1]), previous)
 
     def gather(items):
         half = lax.all_gather(items, "col", axis=1, tiled=True)
@@ -304,8 +304,8 @@
         return weight_both(half, members), *own_part(0, query, left, pair_0)
 
     def last_early(members, items, half, query, left, pair_0):
-        own_0 = own_part(0, query, left, pair_0)
-        return weight_both(gather(after(items, own_0[1])), members), *own_0
+        half = gather(items)
+        return weight_both(half, members), *own_part(0, after(query, half), left, pair_0)
 
     full, *own_0 = by_frame(
         last_late, last_early, after(items, part_0), half, query, left, pair_0

time: 81.2 us -> 79.5 us (0.979)
  starting transfers between devices: 40.1 us -> 39 us
    ppermute x8, starting transfers between devices: 40.1 us -> 39 us  [routed(): return lax.ppermute(block, AXES, route)]
  transfers between devices with their start and end apart: 8 -> 8, of which waited for: 2 -> 2; matrix products, arithmetic and copies ran while one was open for 0% -> 0% of each run, Pallas kernels for 20% -> 21%
where the time goes in v3:
time: 79.5 us; the launch traced here: 79 us
  starting transfers between devices  39 us (49%)
  Pallas kernels  18 us (23%)
  blocking collectives  13.7 us (17%)
  waiting for transfers between devices  5.66 us (7%)
  local copies, waits for them, and re-layouts  2.19 us (3%)
    ppermute x8, starting transfers between devices, routed(): return lax.ppermute(block, AXES, route)  39 us
    all_gather x1, blocking collectives, gather(): half = lax.all_gather(items, 'col', axis=1, tiled=True)  13.7 us
    pallas_call x2, Pallas kernels, own_part(): call(functools.partial(own_kernel, col), (jax.ShapeDtypeStruct((CHANNELS,...  7.42 us
    pallas_call x2, Pallas kernels, upper_part(): call(kernel, jax.ShapeDtypeStruct((PACKED, TOKENS), jnp.bfloat16), (pltpu...  7.13 us
    ppermute x8, waiting for transfers between devices, routed(): return lax.ppermute(block, AXES, route)  5.66 us
    pallas_call x2, Pallas kernels, project(): call(project_kernel, jax.ShapeDtypeStruct(shape, jnp.bfloat16), (pltpu.VM...  3.19 us
    unnamed x12, local copies, waits for them, and re-layouts  2.19 us
  transfers between devices with their start and end apart: 8, of which 2 were waited for; matrix products, arithmetic and copies ran while one was open for 0% of the time, Pallas kernels for 21%

profile of v3, /device:TPU:1, one launch (start us, length us, event | category | flops | bytes accessed | tf_op | source)
XLA Modules:
  0.0 79.0 jit_solution(820143120211890399)
XLA Ops:
  0.0 9.6 %collective-permute-start.3 = (bf16[40,640]{1,0:T(8,128)(2,1)}, bf16[40,640]{1,0:T(8,128)(2,1)S(1)}, u32[]{:S(2)}, u32[]{:S(2)}) collective-permute-start(bf16[40,640]{1,0:T(8,128)(2,1)} %bitcast.5), channel_id=1, source_target_pairs={{0,8},{1,9},{2,10},{3,11},{4,12},{5,13},{6,14},{7,15},{8,16},{9,17... | collective-permute-start | bytes 153608 | tf_op jit(solution)/shard_map/ppermute | solution.py:37
  9.6 5.6 %collective-permute-start.2 = (bf16[40,640]{1,0:T(8,128)(2,1)}, bf16[40,640]{1,0:T(8,128)(2,1)S(1)}, u32[]{:S(2)}, u32[]{:S(2)}) collective-permute-start(bf16[40,640]{1,0:T(8,128)(2,1)} %bitcast.6), channel_id=1, source_target_pairs={{0,24},{1,25},{2,26},{3,27},{4,28},{5,29},{6,30},{7,31},{8,0},{9,1... | collective-permute-start | bytes 153608 | tf_op jit(solution)/shard_map/ppermute | solution.py:37
  15.2 3.3 %collective-permute-start.5 = (bf16[16,32,640]{2,1,0:T(8,128)(2,1)}, bf16[16,32,640]{2,1,0:T(8,128)(2,1)S(1)}, u32[]{:S(2)}, u32[]{:S(2)}) collective-permute-start(bf16[16,32,640]{2,1,0:T(8,128)(2,1)} %query.1), channel_id=1, source_target_pairs={{4,0},{5,1},{6,2},{7,3},{8,4},{9,5},{10,6},{11,7},{12,8},{13,9},{1... | collective-permute-start | bytes 1966088 | tf_op jit(solution)/shard_map/ppermute | solution.py:37
  18.6 1.1 %copy-done = bf16[16,32,640]{2,1,0:T(8,128)(2,1)S(1)} copy-done((bf16[16,32,640]{2,1,0:T(8,128)(2,1)S(1)}, bf16[16,32,640]{2,1,0:T(8,128)(2,1)}, u32[]{:S(2)}) %copy-start) | copy-done | bytes 655384
  19.6 1.1 %copy-done.1 = bf16[16,32,640]{2,1,0:T(8,128)(2,1)S(1)} copy-done((bf16[16,32,640]{2,1,0:T(8,128)(2,1)S(1)}, bf16[16,32,640]{2,1,0:T(8,128)(2,1)}, u32[]{:S(2)}) %copy-start.1) | copy-done | bytes 655384
  20.7 0.1 pair.1
  20.8 3.8 %collective-permute-start.6 = (bf16[32,16,640]{2,1,0:T(8,128)(2,1)S(1)}, bf16[32,16,640]{2,1,0:T(8,128)(2,1)}, u32[]{:S(2)}, u32[]{:S(2)}) collective-permute-start(bf16[32,16,640]{2,1,0:T(8,128)(2,1)S(1)} %get-tuple-element.48.pair_b), channel_id=1, source_target_pairs={{0,1},{1,2},{2,3},{4,5},{5,6},{6,7},{8,9},{9,10},{10,11},{12,13},{... | collective-permute-start | bytes 1966088 | tf_op jit(solution)/shard_map/ppermute | solution.py:37
  24.6 5.2 %collective-permute-start.4 = (bf16[40,640]{1,0:T(8,128)(2,1)S(1)}, bf16[40,640]{1,0:T(8,128)(2,1)S(1)}, u32[]{:S(2)}, u32[]{:S(2)}) collective-permute-start(bf16[40,640]{1,0:T(8,128)(2,1)S(1)} %collective-permute-done.3.refs_3_), channel_id=1, source_target_pairs={{0,8},{1,9},{2,10},{3,11},{4,12},{5,13},{6,14},{7,15},{8,16},{9,17... | collective-permute-start | bytes 153608 | tf_op jit(solution)/shard_map/ppermute | solution.py:37
  29.8 3.2 %own_1.1 = (f32[640,256]{1,0:T(8,128)S(1)}, f32[16,256]{1,0:T(8,128)S(1)}) custom-call(bf16[16,32,640]{2,1,0:T(8,128)(2,1)S(1)} %copy-done.4, bf16[32,16,640]{2,1,0:T(8,128)(2,1)S(1)} %get-tuple-element.50.pair_a.pair_b, bf16[32,16,640]{2,1,0:T(8,128)(2,1)S(1)} %get-tuple-element.48.pair_b), custom_call_target="tpu_custom_call" | custom-call | flops 1024 | bytes 1024 | tf_op jit(solution)/shard_map/own_1/pallas_call | solution.py:189
  33.0 1.0 %collective-permute-done.4.refs_2_ = bf16[40,640]{1,0:T(8,128)(2,1)S(1)} collective-permute-done((bf16[40,640]{1,0:T(8,128)(2,1)S(1)}, bf16[40,640]{1,0:T(8,128)(2,1)S(1)}, u32[]{:S(2)}, u32[]{:S(2)}) %collective-permute-start.4) | collective-permute-done | bytes 51232 | tf_op jit(solution)/shard_map/ppermute | solution.py:37
  34.0 13.7 %conditional.2 = (bf16[640,640]{1,0:T(8,128)(2,1)}) conditional(s32[]{:T(128)} %convert_element_type.4, () %tuple.25, bf16[4,40,640]{2,1,0:T(8,128)(2,1)S(1)} %stack.1), branch_computations={%region_0.0_spmd, %region_1.0_spmd} | conditional | bytes 1024008 | solution.py:259
  34.0 13.7 %all_gather.4 = bf16[4,160,640]{2,1,0:T(8,128)(2,1)} all-gather(bf16[4,40,640]{2,1,0:T(8,128)(2,1)S(1)} %param.1), channel_id=1, replica_groups=mesh['frame'=16,'row'=8,'col'=4] {'col'}, dimensions={1}, use_global_device_ids=true | all-gather | bytes 1024000 | tf_op jit(solution)/shard_map/cond/branch_1_fun/all_gather | solution.py:288
  47.7 4.6 %collective-permute-done.5.query = bf16[16,32,640]{2,1,0:T(8,128)(2,1)S(1)} collective-permute-done((bf16[16,32,640]{2,1,0:T(8,128)(2,1)}, bf16[16,32,640]{2,1,0:T(8,128)(2,1)S(1)}, u32[]{:S(2)}, u32[]{:S(2)}) %collective-permute-start.5) | collective-permute-done | bytes 655392 | tf_op jit(solution)/shard_map/ppermute | solution.py:37
  52.3 3.0 %part_1.1.refs_0_ = bf16[672,256]{1,0:T(8,128)(2,1)S(1)} custom-call(bf16[16,32,640]{2,1,0:T(8,128)(2,1)S(1)} %collective-permute-done.5.query, bf16[32,16,640]{2,1,0:T(8,128)(2,1)S(1)} %get-tuple-element.50.pair_a.pair_b, bf16[32,16,640]{2,1,0:T(8,128)(2,1)S(1)} %get-tuple-element.48.pair_b, bf16[640,640]{1,0:T(8,128)(2,1)} %get-tuple-element.64.refs_0_), custom_call_target="tpu_custom_call" | custom-call | flops 1024 | bytes 1024 | tf_op jit(solution)/shard_map/part_1/pallas_call | solution.py:204
  55.3 0.0 copy-start.5
  55.3 6.5 %collective-permute-start.8 = (bf16[672,256]{1,0:T(8,128)(2,1)S(1)}, bf16[672,256]{1,0:T(8,128)(2,1)S(1)}, u32[]{:S(2)}, u32[]{:S(2)}) collective-permute-start(bf16[672,256]{1,0:T(8,128)(2,1)S(1)} %part_1.1.refs_0_), channel_id=1, source_target_pairs={{0,4},{1,5},{2,6},{3,7},{4,8},{5,9},{6,10},{7,11},{8,12},{9,13},{1... | collective-permute-start | bytes 1032200 | tf_op jit(solution)/shard_map/ppermute | solution.py:37
  61.8 4.1 %part_0.1 = bf16[672,256]{1,0:T(8,128)(2,1)S(1)} custom-call(bf16[16,32,640]{2,1,0:T(8,128)(2,1)S(1)} %collective-permute-done.5.query, bf16[32,16,640]{2,1,0:T(8,128)(2,1)} %collective-permute-done.6.pair_a, bf16[32,16,640]{2,1,0:T(8,128)(2,1)S(1)} %get-tuple-element.50.pair_a.pair_b, bf16[672,256]{1,0:T(8,128)(2,1)S(1)} %part_1.1.refs_0_), custom_call_target="tpu_custom_call" | custom-call | flops 1024 | bytes 1024 | tf_op jit(solution)/shard_map/part_0/pallas_call | solution.py:204
  66.0 3.0 %collective-permute-start.7 = (bf16[672,256]{1,0:T(8,128)(2,1)S(1)}, bf16[672,256]{1,0:T(8,128)(2,1)S(1)}, u32[]{:S(2)}, u32[]{:S(2)}) collective-permute-start(bf16[672,256]{1,0:T(8,128)(2,1)S(1)} %part_0.1), channel_id=1, source_target_pairs={{0,4},{1,5},{2,6},{3,7},{4,8},{5,9},{6,10},{7,11},{8,12},{9,13},{1... | collective-permute-start | bytes 1032200 | tf_op jit(solution)/shard_map/ppermute | solution.py:37
  69.0 6.8 %conditional.3 = (bf16[1280,640]{1,0:T(8,128)(2,1)S(1)}, f32[640,256]{1,0:T(8,128)S(1)}, f32[16,256]{1,0:T(8,128)S(1)}) conditional(s32[]{:T(128)} %convert_element_type.4, (bf16[4,40,640]{2,1,0:T(8,128)(2,1)S(1)}, bf16[16,32,640]{2,1,0:T(8,128)(2,1)S(1)}, bf16[32,16,640]{2,1,0:T(8,128)(2,1)}, bf16[32,16,640]{2,1,0:T(8,128)(2,1)S(1)}) %tuple.34, ...), branch_computations={%region_2.0_spmd, %region_3.0_spmd} | conditional | flops 1024 | bytes 4302912 | solution.py:259
  69.0 2.1 %collective-permute-start.1 = (bf16[640,640]{1,0:T(8,128)(2,1)S(1)}, bf16[640,640]{1,0:T(8,128)(2,1)S(1)}, u32[]{:S(2)}, u32[]{:S(2)}) collective-permute-start(bf16[640,640]{1,0:T(8,128)(2,1)S(1)} %get-tuple-element.32.weight), channel_id=1, source_target_pairs={{0,4},{1,5},{2,6},{3,7},{4,0},{5,1},{6,2},{7,3},{8,12},{9,13},{10,... | collective-permute-start | bytes 2457608 | tf_op jit(solution)/shard_map/cond/branch_1_fun/ppermute | solution.py:37
  71.1 4.3 %own_0.3 = (f32[640,256]{1,0:T(8,128)S(1)}, f32[16,256]{1,0:T(8,128)S(1)}) custom-call(bf16[16,32,640]{2,1,0:T(8,128)(2,1)S(1)} %get-tuple-element.33.query, bf16[32,16,640]{2,1,0:T(8,128)(2,1)} %get-tuple-element.34.pair_a, bf16[32,16,640]{2,1,0:T(8,128)(2,1)S(1)} %get-tuple-element.35.pair_b), custom_call_target="tpu_custom_call" | custom-call | flops 1024 | bytes 1024 | tf_op jit(solution)/shard_map/cond/branch_1_fun/own_0/pallas_call | solution.py:189
  75.4 0.2 order.3
  75.8 1.6 %project_1.1.refs_0_ = bf16[16,32,1280]{2,1,0:T(8,128)(2,1)} custom-call(f32[640,256]{1,0:T(8,128)S(1)} %get-tuple-element.57.mixed, f32[16,256]{1,0:T(8,128)S(1)} %get-tuple-element.51.stats, bf16[672,256]{1,0:T(8,128)(2,1)S(1)} %collective-permute-done.8.upper, bf16[1280,640]{1,0:T(8,128)(2,1)S(1)} %get-tuple-element.56.full), custom_call_target="tpu_custom_call" | custom-call | flops 1024 | bytes 1024 | tf_op jit(solution)/shard_map/project_1/pallas_call | solution.py:222
  77.4 1.6 %project_0.1 = bf16[16,32,1280]{2,1,0:T(8,128)(2,1)} custom-call(f32[640,256]{1,0:T(8,128)S(1)} %get-tuple-element.54.mixed, f32[16,256]{1,0:T(8,128)S(1)} %get-tuple-element.55.stats, bf16[672,256]{1,0:T(8,128)(2,1)S(1)} %collective-permute-done.7.upper, bf16[1280,640]{1,0:T(8,128)(2,1)S(1)} %get-tuple-element.56.full, ...), custom_call_target="tpu_custom_call", output_to_operand_aliasing={{}: (4, {})} | custom-call | flops 1024 | bytes 1024 | tf_op jit(solution)/shard_map/project_0/pallas_call | solution.py:222
  (16 shorter events, 0.1 us)
Async XLA Ops:
  0.0 24.6 %collective-permute-start.3 = (bf16[40,640]{1,0:T(8,128)(2,1)}, bf16[40,640]{1,0:T(8,128)(2,1)S(1)}, u32[]{:S(2)}, u32[]{:S(2)}) collective-permute-start(bf16[40,640]{1,0:T(8,128)(2,1)} %bitcast.5), channel_id=1, source_target_pairs={{0,8},{1,9},{2,10},{3,11},{4,12},{5,13},{6,14},{7,15},{8,16},{9,17... | collective-permute-start | bytes 153608 | tf_op jit(solution)/shard_map/ppermute | solution.py:37
  9.6 15.0 %collective-permute-start.2 = (bf16[40,640]{1,0:T(8,128)(2,1)}, bf16[40,640]{1,0:T(8,128)(2,1)S(1)}, u32[]{:S(2)}, u32[]{:S(2)}) collective-permute-start(bf16[40,640]{1,0:T(8,128)(2,1)} %bitcast.6), channel_id=1, source_target_pairs={{0,24},{1,25},{2,26},{3,27},{4,28},{5,29},{6,30},{7,31},{8,0},{9,1... | collective-permute-start | bytes 153608 | tf_op jit(solution)/shard_map/ppermute | solution.py:37
  15.2 37.1 %collective-permute-start.5 = (bf16[16,32,640]{2,1,0:T(8,128)(2,1)}, bf16[16,32,640]{2,1,0:T(8,128)(2,1)S(1)}, u32[]{:S(2)}, u32[]{:S(2)}) collective-permute-start(bf16[16,32,640]{2,1,0:T(8,128)(2,1)} %query.1), channel_id=1, source_target_pairs={{4,0},{5,1},{6,2},{7,3},{8,4},{9,5},{10,6},{11,7},{12,8},{13,9},{1... | collective-permute-start | bytes 1966088 | tf_op jit(solution)/shard_map/ppermute | solution.py:37
  18.6 1.1 %copy-start = (bf16[16,32,640]{2,1,0:T(8,128)(2,1)S(1)}, bf16[16,32,640]{2,1,0:T(8,128)(2,1)}, u32[]{:S(2)}) copy-start(bf16[16,32,640]{2,1,0:T(8,128)(2,1)} %keys.1) | copy-start | bytes 1966084
  19.6 1.1 %copy-start.1 = (bf16[16,32,640]{2,1,0:T(8,128)(2,1)S(1)}, bf16[16,32,640]{2,1,0:T(8,128)(2,1)}, u32[]{:S(2)}) copy-start(bf16[16,32,640]{2,1,0:T(8,128)(2,1)} %values.1) | copy-start | bytes 1966084
  20.7 9.1 %copy-start.4 = (bf16[16,32,640]{2,1,0:T(8,128)(2,1)S(1)}, bf16[16,32,640]{2,1,0:T(8,128)(2,1)}, u32[]{:S(2)}) copy-start(bf16[16,32,640]{2,1,0:T(8,128)(2,1)} %query.1) | copy-start | bytes 1966084
  20.7 13.2 %copy-start.2 = (bf16[640,40]{0,1:T(8,128)(2,1)S(1)}, bf16[640,40]{0,1:T(8,128)(2,1)}, u32[]{:S(2)}) copy-start(bf16[640,40]{0,1:T(8,128)(2,1)} %param.11) | copy-start | bytes 153604
  20.8 41.0 %collective-permute-start.6 = (bf16[32,16,640]{2,1,0:T(8,128)(2,1)S(1)}, bf16[32,16,640]{2,1,0:T(8,128)(2,1)}, u32[]{:S(2)}, u32[]{:S(2)}) collective-permute-start(bf16[32,16,640]{2,1,0:T(8,128)(2,1)S(1)} %get-tuple-element.48.pair_b), channel_id=1, source_target_pairs={{0,1},{1,2},{2,3},{4,5},{5,6},{6,7},{8,9},{9,10},{10,11},{12,13},{... | collective-permute-start | bytes 1966088 | tf_op jit(solution)/shard_map/ppermute | solution.py:37
  24.6 9.4 %collective-permute-start.4 = (bf16[40,640]{1,0:T(8,128)(2,1)S(1)}, bf16[40,640]{1,0:T(8,128)(2,1)S(1)}, u32[]{:S(2)}, u32[]{:S(2)}) collective-permute-start(bf16[40,640]{1,0:T(8,128)(2,1)S(1)} %collective-permute-done.3.refs_3_), channel_id=1, source_target_pairs={{0,8},{1,9},{2,10},{3,11},{4,12},{5,13},{6,14},{7,15},{8,16},{9,17... | collective-permute-start | bytes 153608 | tf_op jit(solution)/shard_map/ppermute | solution.py:37
  55.3 13.7 %copy-start.3 = (bf16[640,640]{1,0:T(8,128)(2,1)S(1)}, bf16[640,640]{1,0:T(8,128)(2,1)}, u32[]{:S(2)}) copy-start(bf16[640,640]{1,0:T(8,128)(2,1)} %get-tuple-element.64.refs_0_) | copy-start | bytes 2457604
  55.3 13.7 %copy-start.5 = (bf16[16,32,640]{2,1,0:T(8,128)(2,1)S(1)}, bf16[16,32,640]{2,1,0:T(8,128)(2,1)}, u32[]{:S(2)}) copy-start(bf16[16,32,640]{2,1,0:T(8,128)(2,1)} %query.1) | copy-start | bytes 1966084
  55.3 20.5 %collective-permute-start.8 = (bf16[672,256]{1,0:T(8,128)(2,1)S(1)}, bf16[672,256]{1,0:T(8,128)(2,1)S(1)}, u32[]{:S(2)}, u32[]{:S(2)}) collective-permute-start(bf16[672,256]{1,0:T(8,128)(2,1)S(1)} %part_1.1.refs_0_), channel_id=1, source_target_pairs={{0,4},{1,5},{2,6},{3,7},{4,8},{5,9},{6,10},{7,11},{8,12},{9,13},{1... | collective-permute-start | bytes 1032200 | tf_op jit(solution)/shard_map/ppermute | solution.py:37
  66.0 11.4 %collective-permute-start.7 = (bf16[672,256]{1,0:T(8,128)(2,1)S(1)}, bf16[672,256]{1,0:T(8,128)(2,1)S(1)}, u32[]{:S(2)}, u32[]{:S(2)}) collective-permute-start(bf16[672,256]{1,0:T(8,128)(2,1)S(1)} %part_0.1), channel_id=1, source_target_pairs={{0,4},{1,5},{2,6},{3,7},{4,8},{5,9},{6,10},{7,11},{8,12},{9,13},{1... | collective-permute-start | bytes 1032200 | tf_op jit(solution)/shard_map/ppermute | solution.py:37
  69.0 6.4 %collective-permute-start.1 = (bf16[640,640]{1,0:T(8,128)(2,1)S(1)}, bf16[640,640]{1,0:T(8,128)(2,1)S(1)}, u32[]{:S(2)}, u32[]{:S(2)}) collective-permute-start(bf16[640,640]{1,0:T(8,128)(2,1)S(1)} %get-tuple-element.32.weight), channel_id=1, source_target_pairs={{0,4},{1,5},{2,6},{3,7},{4,0},{5,1},{6,2},{7,3},{8,12},{9,13},{10,... | collective-permute-start | bytes 2457608 | tf_op jit(solution)/shard_map/cond/branch_1_fun/ppermute | solution.py:37

commit v4 on v3

--- a/solution.py
+++ b/solution.py
@@ -172,7 +172,7 @@
         kernel,
         out_shape=outs,
         scratch_shapes=list(scratch),
-        compiler_params=pltpu.CompilerParams(vmem_limit_bytes=32 * 1024 * 1024),
+        compiler_params=pltpu.CompilerParams(vmem_limit_bytes=20 * 1024 * 1024),
         cost_estimate=pl.CostEstimate(flops=flops, bytes_accessed=1024, transcendentals=0),
         name=name,
         **more,

time: 79.5 us -> 79.5 us (level)
  no operation moved by 1% of the time
where the time goes in v4:
time: 79.5 us; the launch traced here: 79 us
  starting transfers between devices  39 us (49%)
  Pallas kernels  18 us (23%)
  blocking collectives  13.7 us (17%)
  waiting for transfers between devices  5.66 us (7%)
  local copies, waits for them, and re-layouts  2.19 us (3%)
    ppermute x8, starting transfers between devices, routed(): return lax.ppermute(block, AXES, route)  39 us
    all_gather x1, blocking collectives, gather(): half = lax.all_gather(items, 'col', axis=1, tiled=True)  13.7 us
    pallas_call x2, Pallas kernels, own_part(): call(functools.partial(own_kernel, col), (jax.ShapeDtypeStruct((CHANNELS,...  7.42 us
    pallas_call x2, Pallas kernels, upper_part(): call(kernel, jax.ShapeDtypeStruct((PACKED, TOKENS), jnp.bfloat16), (pltpu...  7.13 us
    ppermute x8, waiting for transfers between devices, routed(): return lax.ppermute(block, AXES, route)  5.66 us
    pallas_call x2, Pallas kernels, project(): call(project_kernel, jax.ShapeDtypeStruct(shape, jnp.bfloat16), (pltpu.VM...  3.19 us
    unnamed x12, local copies, waits for them, and re-layouts  2.19 us
  transfers between devices with their start and end apart: 8, of which 2 were waited for; matrix products, arithmetic and copies ran while one was open for 0% of the time, Pallas kernels for 21%

profile of v4, /device:TPU:1, one launch (start us, length us, event | category | flops | bytes accessed | tf_op | source)
XLA Modules:
  0.0 79.0 jit_solution(7702278652014479408)
XLA Ops:
  0.0 9.6 %collective-permute-start.3 = (bf16[40,640]{1,0:T(8,128)(2,1)}, bf16[40,640]{1,0:T(8,128)(2,1)S(1)}, u32[]{:S(2)}, u32[]{:S(2)}) collective-permute-start(bf16[40,640]{1,0:T(8,128)(2,1)} %bitcast.5), channel_id=1, source_target_pairs={{0,8},{1,9},{2,10},{3,11},{4,12},{5,13},{6,14},{7,15},{8,16},{9,17... | collective-permute-start | bytes 153608 | tf_op jit(solution)/shard_map/ppermute | solution.py:37
  9.6 5.6 %collective-permute-start.2 = (bf16[40,640]{1,0:T(8,128)(2,1)}, bf16[40,640]{1,0:T(8,128)(2,1)S(1)}, u32[]{:S(2)}, u32[]{:S(2)}) collective-permute-start(bf16[40,640]{1,0:T(8,128)(2,1)} %bitcast.6), channel_id=1, source_target_pairs={{0,24},{1,25},{2,26},{3,27},{4,28},{5,29},{6,30},{7,31},{8,0},{9,1... | collective-permute-start | bytes 153608 | tf_op jit(solution)/shard_map/ppermute | solution.py:37
  15.2 3.3 %collective-permute-start.5 = (bf16[16,32,640]{2,1,0:T(8,128)(2,1)}, bf16[16,32,640]{2,1,0:T(8,128)(2,1)S(1)}, u32[]{:S(2)}, u32[]{:S(2)}) collective-permute-start(bf16[16,32,640]{2,1,0:T(8,128)(2,1)} %query.1), channel_id=1, source_target_pairs={{4,0},{5,1},{6,2},{7,3},{8,4},{9,5},{10,6},{11,7},{12,8},{13,9},{1... | collective-permute-start | bytes 1966088 | tf_op jit(solution)/shard_map/ppermute | solution.py:37
  18.6 1.1 %copy-done = bf16[16,32,640]{2,1,0:T(8,128)(2,1)S(1)} copy-done((bf16[16,32,640]{2,1,0:T(8,128)(2,1)S(1)}, bf16[16,32,640]{2,1,0:T(8,128)(2,1)}, u32[]{:S(2)}) %copy-start) | copy-done | bytes 655384
  19.6 1.1 %copy-done.1 = bf16[16,32,640]{2,1,0:T(8,128)(2,1)S(1)} copy-done((bf16[16,32,640]{2,1,0:T(8,128)(2,1)S(1)}, bf16[16,32,640]{2,1,0:T(8,128)(2,1)}, u32[]{:S(2)}) %copy-start.1) | copy-done | bytes 655384
  20.7 0.1 pair.1
  20.8 3.8 %collective-permute-start.6 = (bf16[32,16,640]{2,1,0:T(8,128)(2,1)S(1)}, bf16[32,16,640]{2,1,0:T(8,128)(2,1)}, u32[]{:S(2)}, u32[]{:S(2)}) collective-permute-start(bf16[32,16,640]{2,1,0:T(8,128)(2,1)S(1)} %get-tuple-element.48.pair_b), channel_id=1, source_target_pairs={{0,1},{1,2},{2,3},{4,5},{5,6},{6,7},{8,9},{9,10},{10,11},{12,13},{... | collective-permute-start | bytes 1966088 | tf_op jit(solution)/shard_map/ppermute | solution.py:37
  24.6 5.2 %collective-permute-start.4 = (bf16[40,640]{1,0:T(8,128)(2,1)S(1)}, bf16[40,640]{1,0:T(8,128)(2,1)S(1)}, u32[]{:S(2)}, u32[]{:S(2)}) collective-permute-start(bf16[40,640]{1,0:T(8,128)(2,1)S(1)} %collective-permute-done.3.refs_3_), channel_id=1, source_target_pairs={{0,8},{1,9},{2,10},{3,11},{4,12},{5,13},{6,14},{7,15},{8,16},{9,17... | collective-permute-start | bytes 153608 | tf_op jit(solution)/shard_map/ppermute | solution.py:37
  29.8 3.2 %own_1.1 = (f32[640,256]{1,0:T(8,128)S(1)}, f32[16,256]{1,0:T(8,128)S(1)}) custom-call(bf16[16,32,640]{2,1,0:T(8,128)(2,1)S(1)} %copy-done.4, bf16[32,16,640]{2,1,0:T(8,128)(2,1)S(1)} %get-tuple-element.50.pair_a.pair_b, bf16[32,16,640]{2,1,0:T(8,128)(2,1)S(1)} %get-tuple-element.48.pair_b), custom_call_target="tpu_custom_call" | custom-call | flops 1024 | bytes 1024 | tf_op jit(solution)/shard_map/own_1/pallas_call | solution.py:189
  33.0 1.0 %collective-permute-done.4.refs_2_ = bf16[40,640]{1,0:T(8,128)(2,1)S(1)} collective-permute-done((bf16[40,640]{1,0:T(8,128)(2,1)S(1)}, bf16[40,640]{1,0:T(8,128)(2,1)S(1)}, u32[]{:S(2)}, u32[]{:S(2)}) %collective-permute-start.4) | collective-permute-done | bytes 51232 | tf_op jit(solution)/shard_map/ppermute | solution.py:37
  34.0 13.7 %conditional.2 = (bf16[640,640]{1,0:T(8,128)(2,1)}) conditional(s32[]{:T(128)} %convert_element_type.4, () %tuple.25, bf16[4,40,640]{2,1,0:T(8,128)(2,1)S(1)} %stack.1), branch_computations={%region_0.0_spmd, %region_1.0_spmd} | conditional | bytes 1024008 | solution.py:259
  34.0 13.7 %all_gather.4 = bf16[4,160,640]{2,1,0:T(8,128)(2,1)} all-gather(bf16[4,40,640]{2,1,0:T(8,128)(2,1)S(1)} %param.1), channel_id=1, replica_groups=mesh['frame'=16,'row'=8,'col'=4] {'col'}, dimensions={1}, use_global_device_ids=true | all-gather | bytes 1024000 | tf_op jit(solution)/shard_map/cond/branch_1_fun/all_gather | solution.py:288
  47.7 4.6 %collective-permute-done.5.query = bf16[16,32,640]{2,1,0:T(8,128)(2,1)S(1)} collective-permute-done((bf16[16,32,640]{2,1,0:T(8,128)(2,1)}, bf16[16,32,640]{2,1,0:T(8,128)(2,1)S(1)}, u32[]{:S(2)}, u32[]{:S(2)}) %collective-permute-start.5) | collective-permute-done | bytes 655392 | tf_op jit(solution)/shard_map/ppermute | solution.py:37
  52.3 3.0 %part_1.1.refs_0_ = bf16[672,256]{1,0:T(8,128)(2,1)S(1)} custom-call(bf16[16,32,640]{2,1,0:T(8,128)(2,1)S(1)} %collective-permute-done.5.query, bf16[32,16,640]{2,1,0:T(8,128)(2,1)S(1)} %get-tuple-element.50.pair_a.pair_b, bf16[32,16,640]{2,1,0:T(8,128)(2,1)S(1)} %get-tuple-element.48.pair_b, bf16[640,640]{1,0:T(8,128)(2,1)} %get-tuple-element.64.refs_0_), custom_call_target="tpu_custom_call" | custom-call | flops 1024 | bytes 1024 | tf_op jit(solution)/shard_map/part_1/pallas_call | solution.py:204
  55.3 0.0 copy-start.5
  55.3 6.5 %collective-permute-start.8 = (bf16[672,256]{1,0:T(8,128)(2,1)S(1)}, bf16[672,256]{1,0:T(8,128)(2,1)S(1)}, u32[]{:S(2)}, u32[]{:S(2)}) collective-permute-start(bf16[672,256]{1,0:T(8,128)(2,1)S(1)} %part_1.1.refs_0_), channel_id=1, source_target_pairs={{0,4},{1,5},{2,6},{3,7},{4,8},{5,9},{6,10},{7,11},{8,12},{9,13},{1... | collective-permute-start | bytes 1032200 | tf_op jit(solution)/shard_map/ppermute | solution.py:37
  61.8 4.1 %part_0.1 = bf16[672,256]{1,0:T(8,128)(2,1)S(1)} custom-call(bf16[16,32,640]{2,1,0:T(8,128)(2,1)S(1)} %collective-permute-done.5.query, bf16[32,16,640]{2,1,0:T(8,128)(2,1)} %collective-permute-done.6.pair_a, bf16[32,16,640]{2,1,0:T(8,128)(2,1)S(1)} %get-tuple-element.50.pair_a.pair_b, bf16[672,256]{1,0:T(8,128)(2,1)S(1)} %part_1.1.refs_0_), custom_call_target="tpu_custom_call" | custom-call | flops 1024 | bytes 1024 | tf_op jit(solution)/shard_map/part_0/pallas_call | solution.py:204
  66.0 3.0 %collective-permute-start.7 = (bf16[672,256]{1,0:T(8,128)(2,1)S(1)}, bf16[672,256]{1,0:T(8,128)(2,1)S(1)}, u32[]{:S(2)}, u32[]{:S(2)}) collective-permute-start(bf16[672,256]{1,0:T(8,128)(2,1)S(1)} %part_0.1), channel_id=1, source_target_pairs={{0,4},{1,5},{2,6},{3,7},{4,8},{5,9},{6,10},{7,11},{8,12},{9,13},{1... | collective-permute-start | bytes 1032200 | tf_op jit(solution)/shard_map/ppermute | solution.py:37
  69.0 6.8 %conditional.3 = (bf16[1280,640]{1,0:T(8,128)(2,1)S(1)}, f32[640,256]{1,0:T(8,128)S(1)}, f32[16,256]{1,0:T(8,128)S(1)}) conditional(s32[]{:T(128)} %convert_element_type.4, (bf16[4,40,640]{2,1,0:T(8,128)(2,1)S(1)}, bf16[16,32,640]{2,1,0:T(8,128)(2,1)S(1)}, bf16[32,16,640]{2,1,0:T(8,128)(2,1)}, bf16[32,16,640]{2,1,0:T(8,128)(2,1)S(1)}) %tuple.34, ...), branch_computations={%region_2.0_spmd, %region_3.0_spmd} | conditional | flops 1024 | bytes 4302912 | solution.py:259
  69.0 2.1 %collective-permute-start.1 = (bf16[640,640]{1,0:T(8,128)(2,1)S(1)}, bf16[640,640]{1,0:T(8,128)(2,1)S(1)}, u32[]{:S(2)}, u32[]{:S(2)}) collective-permute-start(bf16[640,640]{1,0:T(8,128)(2,1)S(1)} %get-tuple-element.32.weight), channel_id=1, source_target_pairs={{0,4},{1,5},{2,6},{3,7},{4,0},{5,1},{6,2},{7,3},{8,12},{9,13},{10,... | collective-permute-start | bytes 2457608 | tf_op jit(solution)/shard_map/cond/branch_1_fun/ppermute | solution.py:37
  71.1 4.3 %own_0.3 = (f32[640,256]{1,0:T(8,128)S(1)}, f32[16,256]{1,0:T(8,128)S(1)}) custom-call(bf16[16,32,640]{2,1,0:T(8,128)(2,1)S(1)} %get-tuple-element.33.query, bf16[32,16,640]{2,1,0:T(8,128)(2,1)} %get-tuple-element.34.pair_a, bf16[32,16,640]{2,1,0:T(8,128)(2,1)S(1)} %get-tuple-element.35.pair_b), custom_call_target="tpu_custom_call" | custom-call | flops 1024 | bytes 1024 | tf_op jit(solution)/shard_map/cond/branch_1_fun/own_0/pallas_call | solution.py:189
  75.4 0.2 order.3
  75.8 1.6 %project_1.1.refs_0_ = bf16[16,32,1280]{2,1,0:T(8,128)(2,1)} custom-call(f32[640,256]{1,0:T(8,128)S(1)} %get-tuple-element.57.mixed, f32[16,256]{1,0:T(8,128)S(1)} %get-tuple-element.51.stats, bf16[672,256]{1,0:T(8,128)(2,1)S(1)} %collective-permute-done.8.upper, bf16[1280,640]{1,0:T(8,128)(2,1)S(1)} %get-tuple-element.56.full), custom_call_target="tpu_custom_call" | custom-call | flops 1024 | bytes 1024 | tf_op jit(solution)/shard_map/project_1/pallas_call | solution.py:222
  77.4 1.6 %project_0.1 = bf16[16,32,1280]{2,1,0:T(8,128)(2,1)} custom-call(f32[640,256]{1,0:T(8,128)S(1)} %get-tuple-element.54.mixed, f32[16,256]{1,0:T(8,128)S(1)} %get-tuple-element.55.stats, bf16[672,256]{1,0:T(8,128)(2,1)S(1)} %collective-permute-done.7.upper, bf16[1280,640]{1,0:T(8,128)(2,1)S(1)} %get-tuple-element.56.full, ...), custom_call_target="tpu_custom_call", output_to_operand_aliasing={{}: (4, {})} | custom-call | flops 1024 | bytes 1024 | tf_op jit(solution)/shard_map/project_0/pallas_call | solution.py:222
  (16 shorter events, 0.1 us)
Async XLA Ops:
  0.0 24.6 %collective-permute-start.3 = (bf16[40,640]{1,0:T(8,128)(2,1)}, bf16[40,640]{1,0:T(8,128)(2,1)S(1)}, u32[]{:S(2)}, u32[]{:S(2)}) collective-permute-start(bf16[40,640]{1,0:T(8,128)(2,1)} %bitcast.5), channel_id=1, source_target_pairs={{0,8},{1,9},{2,10},{3,11},{4,12},{5,13},{6,14},{7,15},{8,16},{9,17... | collective-permute-start | bytes 153608 | tf_op jit(solution)/shard_map/ppermute | solution.py:37
  9.6 15.0 %collective-permute-start.2 = (bf16[40,640]{1,0:T(8,128)(2,1)}, bf16[40,640]{1,0:T(8,128)(2,1)S(1)}, u32[]{:S(2)}, u32[]{:S(2)}) collective-permute-start(bf16[40,640]{1,0:T(8,128)(2,1)} %bitcast.6), channel_id=1, source_target_pairs={{0,24},{1,25},{2,26},{3,27},{4,28},{5,29},{6,30},{7,31},{8,0},{9,1... | collective-permute-start | bytes 153608 | tf_op jit(solution)/shard_map/ppermute | solution.py:37
  15.2 37.1 %collective-permute-start.5 = (bf16[16,32,640]{2,1,0:T(8,128)(2,1)}, bf16[16,32,640]{2,1,0:T(8,128)(2,1)S(1)}, u32[]{:S(2)}, u32[]{:S(2)}) collective-permute-start(bf16[16,32,640]{2,1,0:T(8,128)(2,1)} %query.1), channel_id=1, source_target_pairs={{4,0},{5,1},{6,2},{7,3},{8,4},{9,5},{10,6},{11,7},{12,8},{13,9},{1... | collective-permute-start | bytes 1966088 | tf_op jit(solution)/shard_map/ppermute | solution.py:37
  18.6 1.1 %copy-start = (bf16[16,32,640]{2,1,0:T(8,128)(2,1)S(1)}, bf16[16,32,640]{2,1,0:T(8,128)(2,1)}, u32[]{:S(2)}) copy-start(bf16[16,32,640]{2,1,0:T(8,128)(2,1)} %keys.1) | copy-start | bytes 1966084
  19.6 1.1 %copy-start.1 = (bf16[16,32,640]{2,1,0:T(8,128)(2,1)S(1)}, bf16[16,32,640]{2,1,0:T(8,128)(2,1)}, u32[]{:S(2)}) copy-start(bf16[16,32,640]{2,1,0:T(8,128)(2,1)} %values.1) | copy-start | bytes 1966084
  20.7 9.1 %copy-start.4 = (bf16[16,32,640]{2,1,0:T(8,128)(2,1)S(1)}, bf16[16,32,640]{2,1,0:T(8,128)(2,1)}, u32[]{:S(2)}) copy-start(bf16[16,32,640]{2,1,0:T(8,128)(2,1)} %query.1) | copy-start | bytes 1966084
  20.7 13.2 %copy-start.2 = (bf16[640,40]{0,1:T(8,128)(2,1)S(1)}, bf16[640,40]{0,1:T(8,128)(2,1)}, u32[]{:S(2)}) copy-start(bf16[640,40]{0,1:T(8,128)(2,1)} %param.11) | copy-start | bytes 153604
  20.8 41.0 %collective-permute-start.6 = (bf16[32,16,640]{2,1,0:T(8,128)(2,1)S(1)}, bf16[32,16,640]{2,1,0:T(8,128)(2,1)}, u32[]{:S(2)}, u32[]{:S(2)}) collective-permute-start(bf16[32,16,640]{2,1,0:T(8,128)(2,1)S(1)} %get-tuple-element.48.pair_b), channel_id=1, source_target_pairs={{0,1},{1,2},{2,3},{4,5},{5,6},{6,7},{8,9},{9,10},{10,11},{12,13},{... | collective-permute-start | bytes 1966088 | tf_op jit(solution)/shard_map/ppermute | solution.py:37
  24.6 9.4 %collective-permute-start.4 = (bf16[40,640]{1,0:T(8,128)(2,1)S(1)}, bf16[40,640]{1,0:T(8,128)(2,1)S(1)}, u32[]{:S(2)}, u32[]{:S(2)}) collective-permute-start(bf16[40,640]{1,0:T(8,128)(2,1)S(1)} %collective-permute-done.3.refs_3_), channel_id=1, source_target_pairs={{0,8},{1,9},{2,10},{3,11},{4,12},{5,13},{6,14},{7,15},{8,16},{9,17... | collective-permute-start | bytes 153608 | tf_op jit(solution)/shard_map/ppermute | solution.py:37
  55.3 13.7 %copy-start.3 = (bf16[640,640]{1,0:T(8,128)(2,1)S(1)}, bf16[640,640]{1,0:T(8,128)(2,1)}, u32[]{:S(2)}) copy-start(bf16[640,640]{1,0:T(8,128)(2,1)} %get-tuple-element.64.refs_0_) | copy-start | bytes 2457604
  55.3 13.7 %copy-start.5 = (bf16[16,32,640]{2,1,0:T(8,128)(2,1)S(1)}, bf16[16,32,640]{2,1,0:T(8,128)(2,1)}, u32[]{:S(2)}) copy-start(bf16[16,32,640]{2,1,0:T(8,128)(2,1)} %query.1) | copy-start | bytes 1966084
  55.3 20.5 %collective-permute-start.8 = (bf16[672,256]{1,0:T(8,128)(2,1)S(1)}, bf16[672,256]{1,0:T(8,128)(2,1)S(1)}, u32[]{:S(2)}, u32[]{:S(2)}) collective-permute-start(bf16[672,256]{1,0:T(8,128)(2,1)S(1)} %part_1.1.refs_0_), channel_id=1, source_target_pairs={{0,4},{1,5},{2,6},{3,7},{4,8},{5,9},{6,10},{7,11},{8,12},{9,13},{1... | collective-permute-start | bytes 1032200 | tf_op jit(solution)/shard_map/ppermute | solution.py:37
  66.0 11.4 %collective-permute-start.7 = (bf16[672,256]{1,0:T(8,128)(2,1)S(1)}, bf16[672,256]{1,0:T(8,128)(2,1)S(1)}, u32[]{:S(2)}, u32[]{:S(2)}) collective-permute-start(bf16[672,256]{1,0:T(8,128)(2,1)S(1)} %part_0.1), channel_id=1, source_target_pairs={{0,4},{1,5},{2,6},{3,7},{4,8},{5,9},{6,10},{7,11},{8,12},{9,13},{1... | collective-permute-start | bytes 1032200 | tf_op jit(solution)/shard_map/ppermute | solution.py:37
  69.0 6.4 %collective-permute-start.1 = (bf16[640,640]{1,0:T(8,128)(2,1)S(1)}, bf16[640,640]{1,0:T(8,128)(2,1)S(1)}, u32[]{:S(2)}, u32[]{:S(2)}) collective-permute-start(bf16[640,640]{1,0:T(8,128)(2,1)S(1)} %get-tuple-element.32.weight), channel_id=1, source_target_pairs={{0,4},{1,5},{2,6},{3,7},{4,0},{5,1},{6,2},{7,3},{8,12},{9,13},{10,... | collective-permute-start | bytes 2457608 | tf_op jit(solution)/shard_map/cond/branch_1_fun/ppermute | solution.py:37
